TPU v7x, 256 devices: a whole 4x4x8 slice. The times are simulated.
256 devices in a mesh: dp: 64 (over x, z, core), segment: 4 (over y).
Axes of the slice: x: 4, y: 4, z: 8, core: 2. Of those that a mesh axis runs over, the one named last changes fastest.
Arguments:
- queries_in: bfloat16 [64, 64, 3584], P('dp'), may hold values from -6 to 6
- passages_in: bfloat16 [64, 64, 3584], P('dp'), may hold values from -6 to 6
- query_len: int32 [64], P('dp'), may hold values from 16 to 64
- passage_len: int32 [64], P('dp'), may hold values from 16 to 64
- positive: int32 [64], P('dp'), may hold values from 0 to 63, each once
- norm_gain: float32 [4, 3584], P('segment'), may hold values from 0.5 to 1.5
- w_in: bfloat16 [4, 3584, 1024], P('segment', 'dp'), may hold values from -0.09375 to 0.09375
- w_out: bfloat16 [4, 1024, 3584], P('segment', 'dp'), may hold values from -0.1875 to 0.1875
Outputs:
- query_grads: bfloat16 [4, 64, 64, 3584], P('segment', 'dp')
- passage_grads: bfloat16 [4, 64, 64, 3584], P('segment', 'dp')
- gain_grads: float32 [4, 3584], P('segment')
All inputs are finite; a program needn't handle non-finite values.
Results may differ from a plain program's by a relative error of at most 0.022.
Values may be sent and summed in bfloat16 or wider, within the bound.
A program may use at most 128 MiB of HBM per device.

v0:
```python
import math

import jax
import jax.numpy as jnp
from jax import lax
from jax.sharding import PartitionSpec as P

sharpness_divisor = 0.02


def shifted(array, axis, by):
    devices = lax.axis_size(axis)
    pairs = [(i, i + by) for i in range(devices) if 0 <= i + by < devices]
    return lax.ppermute(array, axis, pairs)


def gelu_slope(pre):
    coeff = math.sqrt(2.0 / math.pi)
    tanh_val = jnp.tanh(coeff * (pre + 0.044715 * pre * pre * pre))
    return 0.5 * (1.0 + tanh_val) + 0.5 * pre * (1.0 - tanh_val * tanh_val) * coeff * (
        1.0 + 3.0 * 0.044715 * pre * pre
    )


def section_forward(stream, w_first, w_second, gain_vec):
    stream_f = stream.astype(jnp.float32)
    scale = lax.rsqrt(jnp.mean(stream_f * stream_f, axis=-1, keepdims=True) + 1e-06)
    normed = (stream_f * scale * gain_vec).astype(jnp.bfloat16)
    pre = jnp.dot(normed, w_first, preferred_element_type=jnp.float32)
    act = jax.nn.gelu(pre, approximate=True).astype(jnp.bfloat16)
    return (stream_f + jnp.dot(act, w_second, preferred_element_type=jnp.float32)).astype(
        jnp.bfloat16
    )


def section_backward(stream, grad_out, w_first, w_second, gain_vec):
    stream_f = stream.astype(jnp.float32)
    scale = lax.rsqrt(jnp.mean(stream_f * stream_f, axis=-1, keepdims=True) + 1e-06)
    normed = (stream_f * scale * gain_vec).astype(jnp.bfloat16)
    pre = jnp.dot(normed, w_first, preferred_element_type=jnp.float32)
    back = jnp.dot(grad_out, w_second.T, preferred_element_type=jnp.float32)
    grad_pre = (back * gelu_slope(pre)).astype(jnp.bfloat16)
    grad_normed = jnp.dot(grad_pre, w_first.T, preferred_element_type=jnp.float32)
    unit = stream_f * scale
    gain_grad = jnp.sum(grad_normed * unit, axis=0)
    grad_unit = grad_normed * gain_vec
    grad_in = grad_out.astype(jnp.float32) + scale * (
        grad_unit - unit * jnp.mean(grad_unit * unit, axis=-1, keepdims=True)
    )
    return (grad_in.astype(jnp.bfloat16), gain_grad)


def local(queries_in, passages_in, query_len, passage_len, positive, norm_gain, w_in, w_out):
    seq_count, length, model_width = queries_in.shape
    row_count = seq_count * length
    segment_at = lax.axis_index("segment")
    segment_total = lax.axis_size("segment")
    gain_vec = norm_gain[0]
    full_first, full_second = (
        lax.all_gather(w_in[0], "dp", axis=0, tiled=True),
        lax.all_gather(w_out[0], "dp", axis=0, tiled=True),
    )
    query_rows = queries_in.reshape(row_count, model_width)
    passage_rows = passages_in.reshape(row_count, model_width)
    batches = [query_rows, passage_rows]
    batch_count = len(batches)
    batch_rows = batches[0].shape[0]
    step_count = segment_total + batch_count - 1

    def run_forward(stream):
        return section_forward(stream, full_first, full_second, gain_vec)

    def pass_along(stream):
        return stream

    kept_inputs = jnp.zeros((batch_count, batch_rows, model_width), jnp.bfloat16)
    outputs = jnp.zeros((batch_count, batch_rows, model_width), jnp.bfloat16)
    incoming = jnp.zeros((batch_rows, model_width), jnp.bfloat16)
    for phase_at in range(step_count):
        if phase_at < batch_count:
            current = jnp.where(segment_at == 0, batches[phase_at], incoming)
        else:
            current = incoming
        slot_at = phase_at - segment_at
        active = (slot_at >= 0) & (slot_at < batch_count)
        place_at = jnp.clip(slot_at, 0, batch_count - 1)
        kept_inputs = jnp.where(
            active, lax.dynamic_update_index_in_dim(kept_inputs, current, place_at, 0), kept_inputs
        )
        result = lax.cond(active, run_forward, pass_along, current)
        outputs = jnp.where(
            active & (segment_at == segment_total - 1),
            lax.dynamic_update_index_in_dim(outputs, result, place_at, 0),
            outputs,
        )
        if phase_at + 1 < step_count:
            incoming = shifted(result, "segment", 1)
    lengths = jnp.concatenate([query_len, passage_len])
    validity_mask = jnp.arange(length, dtype=jnp.int32)[None, :] < lengths[:, None]
    count_totals = lengths.astype(jnp.float32)
    pooled_state = (
        jnp.einsum(
            "np,npi->ni",
            validity_mask.astype(jnp.bfloat16),
            outputs,
            preferred_element_type=jnp.float32,
        )
        / count_totals[:, None]
    )
    inv_norm = lax.rsqrt(jnp.sum(pooled_state * pooled_state, axis=-1) + 1e-06)
    embedded = pooled_state * inv_norm[:, None]
    question_encodings = embedded[:seq_count]
    document_encodings = embedded[seq_count:]
    dp_size = lax.axis_size("dp")
    total_seqs = seq_count * dp_size
    passage_embeddings_all = lax.all_gather(document_encodings, "dp", axis=0, tiled=True)
    similarity_matrix = (
        jnp.dot(question_encodings, passage_embeddings_all.T, precision=lax.Precision.HIGHEST)
        / sharpness_divisor
    )
    top = jnp.max(similarity_matrix, axis=1, keepdims=True)
    expo = jnp.exp(similarity_matrix - top)
    probs = expo / jnp.sum(expo, axis=1, keepdims=True)
    onehot = (jnp.arange(total_seqs, dtype=jnp.int32)[None, :] == positive[:, None]).astype(
        jnp.float32
    )
    similarity_derivative = (probs - onehot) / total_seqs
    question_derivative = (
        jnp.dot(similarity_derivative, passage_embeddings_all, precision=lax.Precision.HIGHEST)
        / sharpness_divisor
    )
    document_derivative = lax.psum_scatter(
        jnp.dot(similarity_derivative.T, question_encodings, precision=lax.Precision.HIGHEST)
        / sharpness_divisor,
        "dp",
        scatter_dimension=0,
        tiled=True,
    )
    grad_emb = jnp.concatenate([question_derivative, document_derivative], axis=0)
    grad_pooled = inv_norm[:, None] * grad_emb - pooled_state * (inv_norm**3)[:, None] * jnp.sum(
        pooled_state * grad_emb, axis=-1, keepdims=True
    )
    weight_rows = validity_mask.astype(jnp.float32) / count_totals[:, None]
    grad_stream = (grad_pooled[:, None, :] * weight_rows[:, :, None]).astype(jnp.bfloat16)
    grad_stream = grad_stream.reshape(2 * row_count, model_width)
    grad_batches = [grad_stream[:row_count], grad_stream[row_count:]]

    def run_backward(pair_in):
        return section_backward(pair_in[0], pair_in[1], full_first, full_second, gain_vec)

    def skip_backward(pair_in):
        return (jnp.zeros_like(pair_in[1]), jnp.zeros((model_width,), jnp.float32))

    grad_buffer = jnp.zeros((batch_count, batch_rows, model_width), jnp.bfloat16)
    gain_sum = jnp.zeros((model_width,), jnp.float32)
    incoming = jnp.zeros((batch_rows, model_width), jnp.bfloat16)
    for phase_at in range(step_count):
        if phase_at < batch_count:
            current = jnp.where(segment_at == segment_total - 1, grad_batches[phase_at], incoming)
        else:
            current = incoming
        slot_at = phase_at - (segment_total - 1 - segment_at)
        active = (slot_at >= 0) & (slot_at < batch_count)
        place_at = jnp.clip(slot_at, 0, batch_count - 1)
        stream_in = lax.dynamic_index_in_dim(kept_inputs, place_at, 0, keepdims=False)
        grad_in, gain_part = lax.cond(active, run_backward, skip_backward, (stream_in, current))
        gain_sum = gain_sum + gain_part
        grad_buffer = jnp.where(
            active, lax.dynamic_update_index_in_dim(grad_buffer, grad_in, place_at, 0), grad_buffer
        )
        if phase_at + 1 < step_count:
            incoming = shifted(grad_in, "segment", -1)
    gain_total = lax.psum(gain_sum, "dp")
    grad_rows = grad_buffer.reshape(2 * row_count, model_width)
    query_out = grad_rows[:row_count].reshape(1, seq_count, length, model_width)
    passage_out = grad_rows[row_count:].reshape(1, seq_count, length, model_width)
    return (query_out, passage_out, gain_total[None, :])


def solution(mesh):
    return jax.shard_map(
        local,
        mesh=mesh,
        in_specs=(
            P("dp", None, None),
            P("dp", None, None),
            P("dp"),
            P("dp"),
            P("dp"),
            P("segment", None),
            P("segment", "dp", None),
            P("segment", "dp", None),
        ),
        out_specs=(
            P("segment", "dp", None, None),
            P("segment", "dp", None, None),
            P("segment", None),
        ),
        check_vma=False,
    )
```

profile of v0, /device:TPU:1, one launch (start us, length us, event | category | flops | bytes accessed | tf_op | source)
XLA Modules:
  0.0 913.9 jit_solution(9711431315865714757)
XLA Ops:
  10.9 1.2 select_dynamic-update-slice_fusion.5
  12.1 85.0 %all-gather.6.cloned.1.call-done = bf16[1,3584,1024]{2,1,0:T(8,128)(2,1)} async-done(((bf16[1,56,1024]{2,1,0:T(8,128)(2,1)}), bf16[1,3584,1024]{2,1,0:T(8,128)(2,1)}) %all-gather.6.cloned.1.call-update) | async-done | bytes 7340048 | tf_op jit(solution)/shard_map/all_gather | solution.py:60
  97.1 81.6 %all-gather.8.cloned.1.call-done = bf16[1,1024,3584]{2,1,0:T(8,128)(2,1)} async-done(((bf16[1,16,3584]{2,1,0:T(8,128)(2,1)}), bf16[1,1024,3584]{2,1,0:T(8,128)(2,1)}) %all-gather.8.cloned.1.call-update) | async-done | bytes 7340048 | tf_op jit(solution)/shard_map/all_gather | solution.py:61
  178.7 8.9 conditional.10
  179.7 7.9 fusion
  187.6 1.3 collective-permute-start
  189.1 9.8 %collective-permute-done = bf16[64,3584]{1,0:T(8,128)(2,1)S(1)} collective-permute-done((bf16[64,3584]{1,0:T(8,128)(2,1)S(1)}, bf16[64,3584]{1,0:T(8,128)(2,1)S(1)}, u32[]{:S(2)}, u32[]{:S(2)}) %collective-permute-start) | collective-permute-done | bytes 458784 | tf_op jit(solution)/shard_map/ppermute | solution.py:14
  199.1 9.0 conditional.11
  200.1 7.9 fusion.30
  208.1 4.1 collective-permute-start.1
  212.4 8.9 collective-permute-done.1
  221.3 13.0 %collective-permute-start.2 = (bf16[64,3584]{1,0:T(8,128)(2,1)S(1)}, bf16[64,3584]{1,0:T(8,128)(2,1)S(1)}, u32[]{:S(2)}, u32[]{:S(2)}) collective-permute-start(bf16[64,3584]{1,0:T(8,128)(2,1)S(1)} %get-tuple-element.404), channel_id=1, source_target_pairs={{0,1},{1,2},{2,3},{4,5},{5,6},{6,7},{8,9},{9,10},{10,11},{12,13},{... | collective-permute-start | bytes 1376264 | tf_op jit(solution)/shard_map/ppermute | solution.py:14
  234.6 7.8 collective-permute-done.2
  242.5 4.1 collective-permute-start.3
  246.9 6.9 collective-permute-done.3
  255.3 52.5 %all-gather.2 = f32[64,1,3584]{2,1,0:T(1,128)S(1)} all-gather(f32[1,1,3584]{2,1,0:T(1,128)S(1)} %get-tuple-element.360), channel_id=1, replica_groups=mesh['dp'=64,'segment'=4] {'dp'}, dimensions={0}, use_global_device_ids=true | all-gather | bytes 931840 | tf_op jit(solution)/shard_map/all_gather | solution.py:116
  307.7 1.4 fusion.399
  309.2 1.2 fusion.397
  310.4 1.3 fusion.396
  311.7 1.1 multiply_multiply_fusion.10
  314.1 197.1 %all-reduce.3.cloned.1.call-done = f32[64,3584]{1,0:T(8,128)} async-done(((f32[64,3584]{1,0:T(8,128)}), f32[64,3584]{1,0:T(8,128)}) %all-reduce.3.cloned.1.call-update) | async-done | bytes 917520
  511.2 1.6 constant_dynamic-slice_fusion
  513.3 0.9 conditional.15
  513.3 0.8 broadcast.469
  514.1 1.3 collective-permute-start.4
  515.6 9.6 %collective-permute-done.4 = bf16[64,3584]{1,0:T(8,128)(2,1)} collective-permute-done((bf16[64,3584]{1,0:T(8,128)(2,1)}, bf16[64,3584]{1,0:T(8,128)(2,1)}, u32[]{:S(2)}, u32[]{:S(2)}) %collective-permute-start.4) | collective-permute-done | bytes 458784 | tf_op jit(solution)/shard_map/ppermute | solution.py:14
  525.2 1.0 conditional.16
  525.2 0.8 broadcast.478
  527.0 1.3 collective-permute-start.5
  528.4 8.6 collective-permute-done.5
  537.0 0.8 conditional.17
  537.8 1.3 collective-permute-start.6
  539.3 60.9 %collective-permute-done.6 = bf16[64,3584]{1,0:T(8,128)(2,1)S(1)} collective-permute-done((bf16[64,3584]{1,0:T(8,128)(2,1)}, bf16[64,3584]{1,0:T(8,128)(2,1)S(1)}, u32[]{:S(2)}, u32[]{:S(2)}) %collective-permute-start.6) | collective-permute-done | bytes 458784 | tf_op jit(solution)/shard_map/ppermute | solution.py:14
  600.2 17.8 %conditional.18 = (bf16[64,3584]{1,0:T(8,128)(2,1)}, f32[3584]{0:T(1024)S(1)}, bf16[1,64,3584]{2,1,0:T(8,128)(2,1)S(1)}) conditional(s32[]{:T(128)} %convert_element_type.239, () %tuple.154, (bf16[64,3584]{1,0:T(8,128)(2,1)S(1)}, bf16[2,64,3584]{2,1,0:T(8,128)(2,1)S(1)}, s32[]{:T(128)}, bf16[1024,3584]{1,0:T(8,128)(2,1)}, ...), branch_computations={%region_35.36_spmd, %region_36.40_spmd} | conditional | flops 1415803392 | bytes 28599084 | solution.py:166
  600.6 5.2 fusion.300
  605.9 10.0 %fusion.298 = (f32[3584]{0:T(1024)S(1)}, f32[64]{0:T(128)S(1)}, f32[64,3584]{1,0:T(8,128)S(1)}) fusion(f32[64]{0:T(128)S(1)} %add_rsqrt_fusion.8, bf16[2,64,3584]{2,1,0:T(8,128)(2,1)S(1)} %get-tuple-element.292, s32[]{:T(128)} %get-tuple-element.293, f32[3584]{0:T(1024)S(1)} %reduce.12, bf16[3584,1024]{1,0:T(8,128)(2,1)} %get-tuple-element.296, ...), kind=kOutput, calls=%fused_computation.305 | convolution fusion | flops 942371264 | bytes 16806404 | tf_op jit(solution)/shard_map/cond/branch_1_fun/dot_general | solution.py:43
  615.8 1.1 fusion.297
  616.9 1.0 copy.75
  617.9 1.3 collective-permute-start.7
  619.2 1.2 select_dynamic-update-slice_fusion.1
  620.4 6.9 collective-permute-done.7
  627.4 18.1 %conditional.19 = (f32[3584]{0:T(1024)}, bf16[1,64,3584]{2,1,0:T(8,128)(2,1)}) conditional(s32[]{:T(128)} %convert_element_type.240, () %tuple.156, (bf16[64,3584]{1,0:T(8,128)(2,1)S(1)}, bf16[1024,3584]{1,0:T(8,128)(2,1)}, bf16[2,64,3584]{2,1,0:T(8,128)(2,1)S(1)}, s32[]{:T(128)}, f32[1,3584]{1,0:T(1,128)S(1)}, ...), branch_computations={%region_40.41_spmd, %region_41.45_spmd} | conditional | flops 1415803392 | bytes 27682624 | solution.py:166
  628.1 4.5 fusion.346
  632.6 10.5 %fusion.339 = (f32[64]{0:T(128)}, f32[3584]{0:T(1024)}, f32[64,3584]{1,0:T(8,128)S(1)}) fusion(f32[3584]{0:T(1024)S(1)} %reduce.13, f32[64]{0:T(128)} %copy-done.5, bf16[2,64,3584]{2,1,0:T(8,128)(2,1)S(1)} %get-tuple-element.299, s32[]{:T(128)} %get-tuple-element.300, bf16[3584,1024]{1,0:T(8,128)(2,1)} %get-tuple-element.302, ...), kind=kOutput, calls=%fused_computation.350 | convolution fusion | flops 942371264 | bytes 16806404 | tf_op jit(solution)/shard_map/cond/branch_1_fun/dot_general | solution.py:43
  643.8 1.7 fusion.345
  646.3 258.7 %psum.7 = f32[1,3584]{1,0:T(1,128)} all-reduce(f32[1,3584]{1,0:T(1,128)S(1)} %broadcast_in_dim.134), channel_id=1, replica_groups=mesh['dp'=64,'segment'=4] {'dp'}, use_global_device_ids=true, to_apply=%region_45.46 | all-reduce | flops 3584 | bytes 28672 | tf_op jit(solution)/shard_map/psum | solution.py:173
  905.0 1.2 select_dynamic-update-slice_fusion
  906.2 1.0 slice_bitcast_fusion
  (82 shorter events, 12.6 us)
Async XLA Ops:
  7.2 89.9 %all-gather.6.cloned.1.call-start = ((), (), s32[]{:S(2)}) async-start(), calls=%async_computation | async-start | bytes 7454720 | tf_op jit(solution)/shard_map/all_gather | solution.py:60
  7.9 170.8 %all-gather.8.cloned.1.call-start = ((), (), s32[]{:S(2)}) async-start(), calls=%async_computation.1 | async-start | bytes 7454720 | tf_op jit(solution)/shard_map/all_gather | solution.py:61
  8.6 502.5 %all-reduce.3.cloned.1.call-start = ((), (), s32[]{:S(2)}) async-start(), calls=%async_computation.2 | async-start | bytes 1835008
  178.7 20.2 %copy-start.4 = (bf16[1,64,3584]{2,1,0:T(8,128)(2,1)S(1)}, bf16[1,64,3584]{2,1,0:T(8,128)(2,1)}, u32[]{:S(2)}) copy-start(bf16[1,64,3584]{2,1,0:T(8,128)(2,1)} %param.29) | copy-start | bytes 1376260
  187.6 11.3 %collective-permute-start = (bf16[64,3584]{1,0:T(8,128)(2,1)S(1)}, bf16[64,3584]{1,0:T(8,128)(2,1)S(1)}, u32[]{:S(2)}, u32[]{:S(2)}) collective-permute-start(bf16[64,3584]{1,0:T(8,128)(2,1)S(1)} %get-tuple-element.402), channel_id=1, source_target_pairs={{0,1},{1,2},{2,3},{4,5},{5,6},{6,7},{8,9},{9,10},{10,11},{12,13},{... | collective-permute-start | bytes 1376264 | tf_op jit(solution)/shard_map/ppermute | solution.py:14
  208.1 13.2 %collective-permute-start.1 = (bf16[64,3584]{1,0:T(8,128)(2,1)S(1)}, bf16[64,3584]{1,0:T(8,128)(2,1)S(1)}, u32[]{:S(2)}, u32[]{:S(2)}) collective-permute-start(bf16[64,3584]{1,0:T(8,128)(2,1)S(1)} %get-tuple-element.403), channel_id=1, source_target_pairs={{0,1},{1,2},{2,3},{4,5},{5,6},{6,7},{8,9},{9,10},{10,11},{12,13},{... | collective-permute-start | bytes 1376264 | tf_op jit(solution)/shard_map/ppermute | solution.py:14
  221.3 21.1 %collective-permute-start.2 = (bf16[64,3584]{1,0:T(8,128)(2,1)S(1)}, bf16[64,3584]{1,0:T(8,128)(2,1)S(1)}, u32[]{:S(2)}, u32[]{:S(2)}) collective-permute-start(bf16[64,3584]{1,0:T(8,128)(2,1)S(1)} %get-tuple-element.404), channel_id=1, source_target_pairs={{0,1},{1,2},{2,3},{4,5},{5,6},{6,7},{8,9},{9,10},{10,11},{12,13},{... | collective-permute-start | bytes 1376264 | tf_op jit(solution)/shard_map/ppermute | solution.py:14
  242.5 11.4 %collective-permute-start.3 = (bf16[64,3584]{1,0:T(8,128)(2,1)S(1)}, bf16[64,3584]{1,0:T(8,128)(2,1)S(1)}, u32[]{:S(2)}, u32[]{:S(2)}) collective-permute-start(bf16[64,3584]{1,0:T(8,128)(2,1)S(1)} %get-tuple-element.405), channel_id=1, source_target_pairs={{0,1},{1,2},{2,3},{4,5},{5,6},{6,7},{8,9},{9,10},{10,11},{12,13},{... | collective-permute-start | bytes 1376264 | tf_op jit(solution)/shard_map/ppermute | solution.py:14
  254.0 58.9 %copy-start.6 = (u32[256]{0:T(256)S(1)}, u32[256]{0:T(256)}, u32[]{:S(2)}) copy-start(u32[256]{0:T(256)} %constant.337) | copy-start | bytes 3076
  254.5 258.7 %copy-start.3 = (f32[1,3584]{1,0:T(1,128)S(1)}, f32[1,3584]{1,0:T(1,128)}, u32[]{:S(2)}) copy-start(f32[1,3584]{1,0:T(1,128)} %param.33) | copy-start | bytes 43012
  514.1 11.1 %collective-permute-start.4 = (bf16[64,3584]{1,0:T(8,128)(2,1)}, bf16[64,3584]{1,0:T(8,128)(2,1)}, u32[]{:S(2)}, u32[]{:S(2)}) collective-permute-start(bf16[64,3584]{1,0:T(8,128)(2,1)} %get-tuple-element.321), channel_id=1, source_target_pairs={{1,0},{2,1},{3,2},{5,4},{6,5},{7,6},{9,8},{10,9},{11,10},{13,12},{... | collective-permute-start | bytes 1376264 | tf_op jit(solution)/shard_map/ppermute | solution.py:14
  526.2 0.8 copy-start
  527.0 10.0 %collective-permute-start.5 = (bf16[64,3584]{1,0:T(8,128)(2,1)}, bf16[64,3584]{1,0:T(8,128)(2,1)S(1)}, u32[]{:S(2)}, u32[]{:S(2)}) collective-permute-start(bf16[64,3584]{1,0:T(8,128)(2,1)} %get-tuple-element.323), channel_id=1, source_target_pairs={{1,0},{2,1},{3,2},{5,4},{6,5},{7,6},{9,8},{10,9},{11,10},{13,12},{... | collective-permute-start | bytes 1376264 | tf_op jit(solution)/shard_map/ppermute | solution.py:14
  537.8 1.3 copy-start.1
  537.8 62.3 %collective-permute-start.6 = (bf16[64,3584]{1,0:T(8,128)(2,1)}, bf16[64,3584]{1,0:T(8,128)(2,1)S(1)}, u32[]{:S(2)}, u32[]{:S(2)}) collective-permute-start(bf16[64,3584]{1,0:T(8,128)(2,1)} %get-tuple-element.325), channel_id=1, source_target_pairs={{1,0},{2,1},{3,2},{5,4},{6,5},{7,6},{9,8},{10,9},{11,10},{13,12},{... | collective-permute-start | bytes 1376264 | tf_op jit(solution)/shard_map/ppermute | solution.py:14
  617.9 1.3 copy-start.2
  617.9 9.4 %collective-permute-start.7 = (bf16[64,3584]{1,0:T(8,128)(2,1)}, bf16[64,3584]{1,0:T(8,128)(2,1)S(1)}, u32[]{:S(2)}, u32[]{:S(2)}) collective-permute-start(bf16[64,3584]{1,0:T(8,128)(2,1)} %get-tuple-element.327), channel_id=1, source_target_pairs={{1,0},{2,1},{3,2},{5,4},{6,5},{7,6},{9,8},{10,9},{11,10},{13,12},{... | collective-permute-start | bytes 1376264 | tf_op jit(solution)/shard_map/ppermute | solution.py:14
  627.6 0.5 copy-start.5
Sparse Core Ops, SparseCore 0:
  10.7 86.2 all-gather.5
  99.8 78.8 all-gather.7
  313.0 198.1 all-reduce.2
where the time goes:
time: 925 us; the launch traced here: 914 us
  waiting for transfers between devices  485 us (52%)
  blocking collectives  311 us (34%)
  matrix products  48.3 us (5%)
  starting transfers between devices  27.8 us (3%)
  other arithmetic  16.4 us (2%)
  between operations  16.3 us (2%)
    psum x1, blocking collectives, local(): gain_total = lax.psum(gain_sum, 'dp')  259 us
    unnamed x4, waiting for transfers between devices  198 us
    ppermute x8, waiting for transfers between devices, shifted(): return lax.ppermute(array, axis, pairs)  119 us
    all_gather x1, waiting for transfers between devices, local(): lax.all_gather(w_in[0], 'dp', axis=0, tiled=True)  85 us
    all_gather x1, waiting for transfers between devices, local(): lax.all_gather(w_out[0], 'dp', axis=0, tiled=True)  81.6 us
    all_gather x1, blocking collectives, local(): lax.all_gather(document_encodings, 'dp', axis=0, tiled=True)  52.5 us
    ppermute x8, starting transfers between devices, shifted(): return lax.ppermute(array, axis, pairs)  27.7 us
    dot_general x2, matrix products, section_backward(): jnp.dot(grad_pre, w_first.T, preferred_element_type=jnp.float32)  20.5 us
  transfers between devices with their start and end apart: 11, of which 11 were waited for; matrix products, arithmetic and copies ran while one was open for 1% of the time, Pallas kernels for 0%

commit v1 on v0

v1 whole, which is shorter than its diff:
```python
import math

import jax
import jax.numpy as jnp
from jax import lax
from jax.experimental import pallas as pl
from jax.experimental.pallas import tpu as pltpu
from jax.sharding import PartitionSpec as P

MESH = pl.DeviceIdType.MESH
BF, F32 = jnp.bfloat16, jnp.float32
HI = lax.Precision.HIGHEST
D, KVW, SEQ, NQ = 3584, 1024, 64, 64
NX, NZ, NC, NY = 4, 8, 2, 4
TEMP = 0.02
CHUNK = 32
CHUNKS = 2 * SEQ // CHUNK
PACK = 512
PACKS = D // PACK
EPS = 1e-06
C0 = math.sqrt(2.0 / math.pi)
W_IN, W_OUT, EMB = 0, 1, 2
ALL = slice(None)
NT = (((1,), (1,)), ((), ()))


def gelu(v):
    return 0.5 * v * (1.0 + jnp.tanh(C0 * (v + 0.044715 * v * v * v)))


def gelu_slope(v):
    t = jnp.tanh(C0 * (v + 0.044715 * v * v * v))
    return 0.5 * (1.0 + t) + 0.5 * v * (1.0 - t * t) * C0 * (1.0 + 3.0 * 0.044715 * v * v)


def kernel(
    tok_ref, gain_ref, weight_ref, pos_ref, wi_ref, wo_ref,
    grad_ref, gsum_ref,
    win, wout, emb, pair, kept, pre, scales, normed, act, outb, gin, dpre, dn, gacc, pooled, dpool,
    near, far,
    ag_send, ag_recv, pair_sem, hop_send, hop_recv, red_send, red_recv,
):
    me = lax.axis_index("dp")
    seg = lax.axis_index("segment")
    x, z, c = me // (NZ * NC), (me // NC) % NZ, me % NC

    def dev(px, pz, pc):
        return ((px * NZ + pz) * NC + pc, seg)

    def xo(by):
        return (x + by + NX) % NX

    def zo(by):
        return (z + by + NZ) % NZ

    barrier = pltpu.get_barrier_semaphore()
    mates = [dev(xo(dx), z, pc) for dx in range(NX) for pc in (c, 1 - c)][1:]
    mates += [dev(x, zo(dz), c) for dz in range(1, NZ)]
    mates += [(me, (seg + by) % NY) for by in (1, NY - 1)]
    for mate in mates:
        pl.semaphore_signal(barrier, inc=1, device_id=mate, device_id_type=MESH)
    pl.semaphore_wait(barrier, len(mates))

    def piece(tensor, colour, xs, zs, pc):
        if tensor == W_IN:
            rows = pl.ds(0, 48) if colour == 0 else pl.ds(48, 64)
            return win.at[xs, zs, rows, pl.ds(pl.multiple_of(pc * 512, 512), 512)]
        if tensor == W_OUT:
            cols = pl.ds(0, 1536) if colour == 0 else pl.ds(1536, 2048)
            return wout.at[xs, zs, pl.ds(pc, 1), :, cols]
        cols = pl.ds(0, 256) if colour == 0 else pl.ds(256, 256)
        return emb.at[xs, zs, pl.ds(pc, 1), :, cols]

    def copy_of(tensor, slot, ref, target):
        return pltpu.make_async_remote_copy(
            src_ref=ref, dst_ref=ref,
            send_sem=ag_send.at[tensor, slot], recv_sem=ag_recv.at[tensor, slot],
            device_id=target, device_id_type=MESH,
        )

    def gather(tensor, colour, plus, pending):
        def send(slot, xs, zs, target):
            op = copy_of(tensor, slot, piece(tensor, colour, xs, zs, c), target)
            op.start()
            pending.append(op.wait_send)

        def got(slot, xs, zs):
            copy_of(tensor, slot, piece(tensor, colour, xs, zs, c), dev(x, z, 1 - c)).wait_recv()

        def pass_on(slot, xs, zs):
            send(slot, xs, zs, dev(x, z, 1 - c))
            other = copy_of(tensor, slot, piece(tensor, colour, xs, zs, 1 - c), dev(x, z, 1 - c))
            pending.append(other.wait_recv)

        def one(at):
            return pl.ds(at, 1)

        up, down = dev(x, zo(1), c), dev(x, zo(-1), c)
        right, left = dev(xo(1), z, c), dev(xo(-1), z, c)
        if colour == 0:
            for dx in range(1, NX):
                send(dx - 1, one(x), one(z), dev(xo(dx), z, c))
            yield
            for dx in range(1, NX):
                got(dx - 1, one(xo(-dx)), one(z))
            send(3, ALL, one(z), up)
            send(4, ALL, one(z), down)
            pass_on(22, ALL, one(z))
            for step in range(1, 4):
                yield
                got(1 + 2 * step, ALL, one(zo(-step)))
                if step < 3:
                    send(3 + 2 * step, ALL, one(zo(-step)), up)
                else:
                    send(9, pl.ds(0, 2), one(zo(-3)), up)
                got(2 + 2 * step, ALL, one(zo(step)))
                if step < 3:
                    send(4 + 2 * step, ALL, one(zo(step)), down)
                else:
                    send(10, pl.ds(2, 2), one(zo(3)), down)
                pass_on(21 + 2 * step, ALL, one(zo(-step)))
                pass_on(22 + 2 * step, ALL, one(zo(step)))
            yield
            got(9, pl.ds(0, 2), one(zo(-4)))
            got(10, pl.ds(2, 2), one(zo(4)))
            pass_on(29, ALL, one(zo(4)))
        else:
            send(11, one(x), one(z), up)
            send(12, one(x), one(z), down)
            for step in range(1, 4):
                yield
                got(9 + 2 * step, one(x), one(zo(-step)))
                if step < 3:
                    send(11 + 2 * step, one(x), one(zo(-step)), up)
                elif plus:
                    send(17, one(x), one(zo(-3)), up)
                got(10 + 2 * step, one(x), one(zo(step)))
                if step < 3:
                    send(12 + 2 * step, one(x), one(zo(step)), down)
                elif not plus:
                    send(17, one(x), one(zo(3)), down)
            yield
            got(17, one(x), one(zo(4)))
            send(18, one(x), ALL, right)
            send(19, one(x), ALL, left)
            pass_on(30, one(x), ALL)
            yield
            got(18, one(xo(-1)), ALL)
            send(20, one(xo(-1)), pl.ds(0, 4), right)
            got(19, one(xo(1)), ALL)
            send(21, one(xo(1)), pl.ds(4, 4), left)
            pass_on(31, one(xo(-1)), ALL)
            pass_on(32, one(xo(1)), ALL)
            yield
            got(20, one(xo(2)), pl.ds(0, 4))
            got(21, one(xo(2)), pl.ds(4, 4))
            pass_on(33, one(xo(2)), ALL)

    def run(streams, ahead=()):
        waiting = list(ahead)
        for stream in streams:
            next(stream)
            waiting.append(stream)
        while waiting:
            for stream in list(waiting):
                if next(stream, "end") == "end":
                    waiting.remove(stream)

    pending = []
    wout[pl.ds(x, 1), pl.ds(z, 1), pl.ds(c, 1)] = wo_ref[...].reshape(1, 1, 1, 16, D)
    first = [gather(W_OUT, 1, False, pending), gather(W_OUT, 0, False, pending)]
    for stream in first:
        next(stream)
    swap = pltpu.make_async_remote_copy(
        src_ref=wi_ref, dst_ref=pair, send_sem=pair_sem.at[0], recv_sem=pair_sem.at[1],
        device_id=dev(x, z, 1 - c), device_id_type=MESH,
    )
    swap.start()

    @pl.when(seg == 0)
    def _():
        kept[...] = tok_ref[...].reshape(2 * SEQ, D)

    swap.wait()
    mine, theirs = wi_ref[...].astype(F32), pair[...].astype(F32)
    both = jnp.concatenate(
        [jnp.where(c == 0, mine, theirs), jnp.where(c == 0, theirs, mine)], axis=0
    )
    half = jnp.where(c == 0, both[:, :512], both[:, 512:]).astype(BF)
    win[pl.ds(x, 1), pl.ds(z, 1), :, pl.ds(pl.multiple_of(c * 512, 512), 512)] = half.reshape(1, 1, 112, 512)
    run([gather(W_IN, 1, True, pending), gather(W_IN, 0, True, pending)], first)
    for wait in pending:
        wait()

    def hop(step, slot, src, dst, to):
        return pltpu.make_async_remote_copy(
            src_ref=src, dst_ref=dst, send_sem=hop_send.at[step, slot], recv_sem=hop_recv.at[step, slot],
            device_id=(me, to), device_id_type=MESH,
        )

    def chunk_rows(k):
        return pl.ds(pl.multiple_of(k * CHUNK, CHUNK), CHUNK)

    gain = gain_ref[...]
    pooled[...] = jnp.zeros_like(pooled)

    @pl.loop(0, CHUNKS)
    def _(k):
        rows = chunk_rows(k)

        @pl.when(seg > 0)
        def _():
            hop(0, k, outb.at[rows], kept.at[rows], seg).wait_recv()

        for part in range(CHUNK // 16):
            sub = pl.ds(pl.multiple_of(k * CHUNK + part * 16, 16), 16)
            stream = kept[sub, :].astype(F32)
            scale = lax.rsqrt(jnp.mean(stream * stream, axis=-1, keepdims=True) + EPS)
            scales[sub, :] = jnp.broadcast_to(scale, (16, 128))
            normed[pl.ds(part * 16, 16), :] = (stream * scale * gain).astype(BF)

        @pl.loop(0, KVW // 256)
        def _(n):
            cols = pl.ds(pl.multiple_of(n * 256, 256), 256)
            v = jnp.dot(normed[...], win[:, :, :, cols].reshape(D, 256), preferred_element_type=F32)
            pre[rows, cols] = v
            act[:, cols] = gelu(v).astype(BF)

        @pl.loop(0, D // 256)
        def _(n):
            cols = pl.ds(pl.multiple_of(n * 256, 256), 256)
            v = jnp.dot(act[...], wout[:, :, :, :, cols].reshape(KVW, 256), preferred_element_type=F32)
            v = (kept[rows, cols].astype(F32) + v).astype(BF)
            outb[rows, cols] = v

        @pl.when(seg < NY - 1)
        def _():
            hop(0, k, outb.at[rows], kept.at[rows], seg + 1).start()

        @pl.when(seg == NY - 1)
        def _():
            half = (k * CHUNK) // SEQ
            total = jnp.zeros((8, D), F32)
            for part in range(CHUNK // 16):
                sub = pl.ds(pl.multiple_of(k * CHUNK + part * 16, 16), 16)
                scaled = outb[sub, :].astype(F32) * weight_ref[sub, 0:1]
                total = total + scaled[0:8] + scaled[8:16]
            pooled[half] += total

    @pl.when(seg == NY - 1)
    def _():
        here = (x, z, c)
        rowsums, invs, packs = [], [], []
        for side in range(2):
            total = jnp.sum(pooled[side], axis=0, keepdims=True)
            inv = lax.rsqrt(jnp.sum(total * total, axis=-1, keepdims=True) + EPS)
            for k in range(PACKS):
                dpool[side, k : k + 1, :] = total[:, k * PACK : (k + 1) * PACK]
            dpool[side, PACKS : PACKS + 1, :] = jnp.zeros((1, PACK), F32)
            packed = dpool[side]
            if side == 0:
                sent = packed * inv + pos_ref[...]
            else:
                sent = packed * inv
            emb[pl.ds(x, 1), pl.ds(z, 1), pl.ds(c, 1), pl.ds(8 * side, 8), :] = sent.reshape(1, 1, 1, 8, PACK)
            invs.append(inv)
            packs.append(packed)
        waits = []
        run([gather(EMB, 1, True, waits), gather(EMB, 0, True, waits)])
        for wait in waits:
            wait()
        q = emb[:, :, :, 0:8, :].reshape(NQ * 8, PACK)
        p = emb[:, :, :, 8:16, :].reshape(NQ * 8, PACK)
        gram = lax.dot_general(q, p, NT, precision=HI, preferred_element_type=F32)
        r = lax.broadcasted_iota(jnp.int32, (NQ * 8, NQ * 8), 0)
        l = lax.broadcasted_iota(jnp.int32, (NQ * 8, NQ * 8), 1)
        gram = jnp.where((r % 8 == l % 8) & (r % 8 < PACKS), gram, 0.0)
        i64 = lax.broadcasted_iota(jnp.int32, (NQ, NQ * 8), 0)
        i512 = lax.broadcasted_iota(jnp.int32, (NQ, NQ * 8), 1)
        fold = jnp.where(i512 // 8 == i64, 1.0, 0.0)
        pick = jnp.where(i512 == i64 * 8 + PACKS, 1.0, 0.0)
        folded = jnp.dot(fold, gram, precision=HI, preferred_element_type=F32)
        logits = lax.dot_general(folded, fold, NT, precision=HI, preferred_element_type=F32) / TEMP
        onehot = jnp.dot(pick, q[:, 0:128], precision=HI, preferred_element_type=F32)[:, 0:NQ]
        expo = jnp.exp(logits - jnp.max(logits, axis=1, keepdims=True))
        probs = expo / jnp.sum(expo, axis=1, keepdims=True)
        dlogits = (probs - onehot) / NQ
        ii = lax.broadcasted_iota(jnp.int32, (NQ, NQ), 0)
        jj = lax.broadcasted_iota(jnp.int32, (NQ, NQ), 1)
        row = jnp.sum(jnp.where(ii == me, dlogits, 0.0), axis=0, keepdims=True)
        col = jnp.sum(jnp.where(jj == me, dlogits, 0.0), axis=1, keepdims=True)
        row = jnp.dot(row, fold, precision=HI, preferred_element_type=F32)
        col = jnp.sum(col * fold, axis=0, keepdims=True)
        k8 = lax.broadcasted_iota(jnp.int32, (8, NQ * 8), 0)
        l8 = lax.broadcasted_iota(jnp.int32, (8, NQ * 8), 1)
        diag = (l8 % 8 == k8) & (k8 < PACKS)
        for side, (spread, other) in enumerate(((row, p), (col, q))):
            demb = jnp.dot(jnp.where(diag, spread, 0.0), other, precision=HI, preferred_element_type=F32) / TEMP
            inv, packed = invs[side], packs[side]
            along = jnp.sum(jnp.sum(packed * demb, axis=1, keepdims=True), axis=0, keepdims=True)
            grad = inv * demb - packed * (inv * inv * inv) * along
            for k in range(PACKS):
                pooled[side, 0:1, k * PACK : (k + 1) * PACK] = grad[k : k + 1, :]
        for side in range(2):
            grad = pooled[side, 0:1, :]
            for part in range(SEQ // 16):
                sub = pl.ds(side * SEQ + part * 16, 16)
                gin[sub, :] = (weight_ref[sub, 0:1] * grad).astype(BF)

    gacc[...] = jnp.zeros_like(gacc)

    @pl.loop(0, CHUNKS)
    def _(k):
        rows = chunk_rows(k)

        @pl.when(seg < NY - 1)
        def _():
            hop(1, k, outb.at[rows], gin.at[rows], seg).wait_recv()
            hop(0, k, outb.at[rows], kept.at[rows], seg).wait_send()

        dout = gin[rows, :]
        for n in range(NX):
            cols = pl.ds(n * 256, 256)
            back = lax.dot_general(dout, wout[n].reshape(256, D), NT, preferred_element_type=F32)
            dpre[:, cols] = (back * gelu_slope(pre[rows, cols])).astype(BF)
        for n in range(NX):
            cols = pl.ds(n * 896, 896)
            dn[:, cols] = lax.dot_general(dpre[...], win[n].reshape(896, KVW), NT, preferred_element_type=F32)
        for part in range(CHUNK // 16):
            sub = pl.ds(pl.multiple_of(k * CHUNK + part * 16, 16), 16)
            scale = scales[sub, 0:1]
            unit = kept[sub, :].astype(F32) * scale
            dnormed = dn[pl.ds(part * 16, 16), :]
            both = dnormed * unit
            gacc[...] += both[0:8] + both[8:16]
            du = dnormed * gain
            mean = jnp.mean(du * unit, axis=-1, keepdims=True)
            res = gin[sub, :].astype(F32) + scale * (du - unit * mean)
            outb[sub, :] = res.astype(BF)

        @pl.when(seg > 0)
        def _():
            hop(1, k, outb.at[rows], gin.at[rows], seg - 1).start()

    grad_ref[...] = outb[...].reshape(2, SEQ, D)

    def reduce(step, buf, slot, at, peers):
        ops = []
        for j, (target, source) in enumerate(peers):
            op = pltpu.make_async_remote_copy(
                src_ref=buf.at[at], dst_ref=buf.at[at],
                send_sem=red_send.at[step, j], recv_sem=red_recv.at[step, j],
                device_id=target, device_id_type=MESH,
            )
            op.start()
            ops.append(op.wait_send)
            ops.append(pltpu.make_async_remote_copy(
                src_ref=buf.at[source], dst_ref=buf.at[source],
                send_sem=red_send.at[step, j], recv_sem=red_recv.at[step, j],
                device_id=target, device_id_type=MESH,
            ).wait_recv)
        for op in ops:
            op()

    at = x * NC + c
    near[at] = jnp.sum(gacc[...], axis=0, keepdims=True)
    peers = []
    for dx in range(NX):
        for other in range(NC):
            if dx or other:
                pc = c if other == 0 else 1 - c
                peers.append((dev(xo(dx), z, pc), xo(-dx) * NC + pc))
    reduce(0, near, 0, at, peers)
    far[z] = jnp.sum(near[...], axis=0)
    reduce(1, far, 0, z, [(dev(x, zo(dz), c), zo(-dz)) for dz in range(1, NZ)])
    gsum_ref[...] = jnp.sum(far[...], axis=0)

    @pl.when(seg > 0)
    def _():
        for k in range(CHUNKS):
            rows = pl.ds(k * CHUNK, CHUNK)
            hop(1, k, outb.at[rows], gin.at[rows], seg).wait_send()


def local(queries_in, passages_in, query_len, passage_len, positive, norm_gain, w_in, w_out):
    tokens = jnp.concatenate([queries_in, passages_in], axis=0)
    lengths = jnp.concatenate([query_len, passage_len])
    mask = (jnp.arange(SEQ, dtype=jnp.int32)[None, :] < lengths[:, None]).astype(F32)
    weights = mask / lengths.astype(F32)[:, None]
    weights = jnp.broadcast_to(weights.reshape(2 * SEQ, 1), (2 * SEQ, 128))
    spot_row = lax.broadcasted_iota(jnp.int32, (8, PACK), 0)
    spot_col = lax.broadcasted_iota(jnp.int32, (8, PACK), 1)
    chosen = ((spot_row == PACKS) & (spot_col == positive[0])).astype(F32)
    vmem = pl.BlockSpec(memory_space=pltpu.VMEM)
    rows = 2 * SEQ
    grads, gains = pl.pallas_call(
        kernel,
        out_shape=(
            jax.ShapeDtypeStruct((2, SEQ, D), BF),
            jax.ShapeDtypeStruct((1, D), F32),
        ),
        in_specs=[vmem] * 6,
        out_specs=(vmem, vmem),
        scratch_shapes=[
            pltpu.VMEM((NX, NZ, 112, KVW), BF),
            pltpu.VMEM((NX, NZ, NC, 16, D), BF),
            pltpu.VMEM((NX, NZ, NC, 16, PACK), F32),
            pltpu.VMEM((56, KVW), BF),
            pltpu.VMEM((rows, D), BF),
            pltpu.VMEM((rows, KVW), F32),
            pltpu.VMEM((rows, 128), F32),
            pltpu.VMEM((CHUNK, D), BF),
            pltpu.VMEM((CHUNK, KVW), BF),
            pltpu.VMEM((rows, D), BF),
            pltpu.VMEM((rows, D), BF),
            pltpu.VMEM((CHUNK, KVW), BF),
            pltpu.VMEM((CHUNK, D), F32),
            pltpu.VMEM((8, D), F32),
            pltpu.VMEM((2, 8, D), F32),
            pltpu.VMEM((2, 8, PACK), F32),
            pltpu.VMEM((NX * NC, 1, D), F32),
            pltpu.VMEM((NZ, 1, D), F32),
            pltpu.SemaphoreType.DMA((3, 34)),
            pltpu.SemaphoreType.DMA((3, 34)),
            pltpu.SemaphoreType.DMA((2,)),
            pltpu.SemaphoreType.DMA((2, CHUNKS)),
            pltpu.SemaphoreType.DMA((2, CHUNKS)),
            pltpu.SemaphoreType.DMA((2, 7)),
            pltpu.SemaphoreType.DMA((2, 7)),
        ],
        compiler_params=pltpu.CompilerParams(
            collective_id=0, has_side_effects=True, vmem_limit_bytes=48 * 1024 * 1024
        ),
        name="embedder_window",
    )(tokens, norm_gain, weights, chosen, w_in[0], w_out[0])
    return grads[0][None, None], grads[1][None, None], gains


def solution(mesh):
    return jax.shard_map(
        local,
        mesh=mesh,
        in_specs=(
            P("dp", None, None),
            P("dp", None, None),
            P("dp"),
            P("dp"),
            P("dp"),
            P("segment", None),
            P("segment", "dp", None),
            P("segment", "dp", None),
        ),
        out_specs=(
            P("segment", "dp", None, None),
            P("segment", "dp", None, None),
            P("segment", None),
        ),
        check_vma=False,
    )
```

time: 925 us -> 224 us (0.24); the launches traced: 914 us -> 223 us
  waiting for transfers between devices: 485 us -> 0 us
  blocking collectives: 311 us -> 0 us
  Pallas kernels: 0 us -> 218 us
  matrix products: 48.3 us -> 0 us
  starting transfers between devices: 27.8 us -> 0 us
  other arithmetic: 16.4 us -> 1.53 us
  between operations: 16.3 us -> 2.64 us
    psum x1 -> x0, blocking collectives: 259 us -> none  [local(): gain_total = lax.psum(gain_sum, 'dp')]
    pallas_call x0 -> x1, Pallas kernels: none -> 218 us  [local(): pl.pallas_call(kernel, out_shape=(jax.ShapeDtypeStruct((2, SEQ, D), BF),...]
    unnamed x4 -> x0, waiting for transfers between devices: 198 us -> none
    all_gather x2 -> x0, waiting for transfers between devices: 167 us -> none  [the longest x1 85 us: local(): lax.all_gather(w_in[0], 'dp', axis=0, tiled=True)]
    ppermute x8 -> x0, waiting for transfers between devices: 119 us -> none  [shifted(): return lax.ppermute(array, axis, pairs)]
    all_gather x1 -> x0, blocking collectives: 52.5 us -> none  [local(): lax.all_gather(document_encodings, 'dp', axis=0, tiled=True)]
    dot_general x9 -> x0, matrix products: 48.3 us -> none  [the longest x2 20.5 us: section_backward(): jnp.dot(grad_pre, w_first.T, preferred_element_type=jnp.float32)]
    ppermute x8 -> x0, starting transfers between devices: 27.7 us -> none  [shifted(): return lax.ppermute(array, axis, pairs)]
  transfers between devices with their start and end apart: 11 -> 0, of which waited for: 11 -> 0; matrix products, arithmetic and copies ran while one was open for 1% -> 0% of each run, Pallas kernels for 0% -> 0%
where the time goes in v1:
time: 224 us; the launch traced here: 223 us
  Pallas kernels  218 us (97%)
  between operations  2.64 us (1%)
    pallas_call x1, Pallas kernels, local(): pl.pallas_call(kernel, out_shape=(jax.ShapeDtypeStruct((2, SEQ, D), BF),...  218 us

profile of v1, /device:TPU:1, one launch (start us, length us, event | category | flops | bytes accessed | tf_op | source)
XLA Modules:
  0.0 223.4 jit_solution(1750854068686378873)
XLA Ops:
  2.6 0.1 fusion.1
  2.7 0.1 fusion
  2.7 0.1 div.17
  2.8 0.1 and_convert_fusion.pos_ref
  2.9 0.1 broadcast_in_dim.2.weight_ref
  3.0 0.0 copy-start
  3.0 0.0 copy-start.1
  3.0 0.0 copy-start.2
  3.0 1.3 pad_maximum_fusion.tok_ref
  4.3 0.0 copy-done
  4.3 0.0 copy-done.1
  4.3 0.0 copy-done.2
  4.3 217.5 %embedder_window.1 = (bf16[2,64,3584]{2,1,0:T(8,128)(2,1)S(1)}, f32[1,3584]{1,0:T(1,128)S(1)}) custom-call(bf16[2,64,3584]{2,1,0:T(8,128)(2,1)S(1)} %pad_maximum_fusion.tok_ref, f32[1,3584]{1,0:T(1,128)S(1)} %copy-done.2, f32[128,128]{1,0:T(8,128)S(1)} %broadcast_in_dim.2.weight_ref, f32[8,512]{1,0:T(8,128)S(1)} %and_convert_fusion.pos_ref, ...), custom_call_target="tpu_custom_call" | custom-call | tf_op jit(solution)/shard_map/embedder_window/pallas_call | solution.py:396
  221.8 1.0 slice_bitcast_fusion
  222.8 0.6 copy.15
  (2 shorter events, 0.0 us)
Async XLA Ops:
  3.0 1.3 copy-start
  3.0 1.3 copy-start.1
  3.0 1.3 copy-start.2

commit v2 on v1

v2 whole, which is shorter than its diff:
```python
import math

import jax
import jax.numpy as jnp
from jax import lax
from jax.experimental import pallas as pl
from jax.experimental.pallas import tpu as pltpu
from jax.sharding import PartitionSpec as P

MESH = pl.DeviceIdType.MESH
BF, F32 = jnp.bfloat16, jnp.float32
HI = lax.Precision.HIGHEST
D, KVW, SEQ, NQ = 3584, 1024, 64, 64
NX, NZ, NC, NY = 4, 8, 2, 4
TEMP = 0.02
CHUNK = 32
CHUNKS = 2 * SEQ // CHUNK
PARTS = 4
WIDE = D // PARTS
PACKS = D // 128
WEIGHT_ORDER = (
    2, 3, 0, 1, 2, 3, 0, 0, 1, 2, 2, 3, 2, 0, 0, 2, 0, 2, 0, 0, 1, 3, 2, 2, 2, 0, 0, 0, 2, 2, 2, 0, 1, 3, 1, 2, 0, 3,
)
EMB_ORDER = (0, 1, 0, 1, 1, 0, 0, 1, 0, 0, 0, 0, 0, 0, 0, 1, 0, 0, 0, 1)
EPS = 1e-06
C0 = math.sqrt(2.0 / math.pi)
W_IN, W_OUT, EMB = 0, 1, 2
ALL = slice(None)
NT = (((1,), (1,)), ((), ()))


def gelu(v):
    return 0.5 * v * (1.0 + jnp.tanh(C0 * (v + 0.044715 * v * v * v)))


def gelu_slope(v):
    t = jnp.tanh(C0 * (v + 0.044715 * v * v * v))
    return 0.5 * (1.0 + t) + 0.5 * v * (1.0 - t * t) * C0 * (1.0 + 3.0 * 0.044715 * v * v)


def kernel(
    queries_ref, passages_ref, gain_ref, weight_ref, pos_ref, wi_ref, wo_ref,
    qgrad_ref, pgrad_ref, gsum_ref,
    win, wout, win_t, wout_t, emb, embs, pair, kept, pre, scales, normed, act, outb, gin, dpre, gacc, pooled,
    pack, near, far,
    ag_send, ag_recv, pair_sem, hop_send, hop_recv, red_send, red_recv,
):
    me = lax.axis_index("dp")
    seg = lax.axis_index("segment")
    x, z, c = me // (NZ * NC), (me // NC) % NZ, me % NC

    def dev(px, pz, pc):
        return ((px * NZ + pz) * NC + pc, seg)

    def xo(by):
        return (x + by + NX) % NX

    def zo(by):
        return (z + by + NZ) % NZ

    barrier = pltpu.get_barrier_semaphore()
    mates = [dev(xo(dx), z, pc) for dx in range(NX) for pc in (c, 1 - c)][1:]
    mates += [dev(x, zo(dz), c) for dz in range(1, NZ)]
    mates += [(me, (seg + by) % NY) for by in (1, NY - 1)]
    for mate in mates:
        pl.semaphore_signal(barrier, inc=1, device_id=mate, device_id_type=MESH)
    pl.semaphore_wait(barrier, len(mates))

    def piece(tensor, colour, xs, zs, pc):
        if tensor == W_IN:
            rows = pl.ds(0, 48) if colour == 0 else pl.ds(48, 64)
            return win.at[xs, zs, rows, pl.ds(pl.multiple_of(pc * 512, 512), 512)]
        if tensor == W_OUT:
            cols = pl.ds(0, 1536) if colour == 0 else pl.ds(1536, 2048)
            return wout.at[xs, zs, pl.ds(pc, 1), :, cols]
        return emb.at[xs, zs, pl.ds(pc, 1), pl.ds(32 * colour, 32), :]

    def copy_of(tensor, slot, ref, target):
        return pltpu.make_async_remote_copy(
            src_ref=ref, dst_ref=ref,
            send_sem=ag_send.at[tensor, slot], recv_sem=ag_recv.at[tensor, slot],
            device_id=target, device_id_type=MESH,
        )

    def gather(tensor, colour, plus, pending):
        def send(slot, xs, zs, target):
            op = copy_of(tensor, slot, piece(tensor, colour, xs, zs, c), target)
            op.start()
            pending.append(op.wait_send)

        def got(slot, xs, zs):
            copy_of(tensor, slot, piece(tensor, colour, xs, zs, c), dev(x, z, 1 - c)).wait_recv()

        def pass_on(slot, xs, zs):
            send(slot, xs, zs, dev(x, z, 1 - c))
            other = copy_of(tensor, slot, piece(tensor, colour, xs, zs, 1 - c), dev(x, z, 1 - c))
            pending.append(other.wait_recv)

        def one(at):
            return pl.ds(at, 1)

        up, down = dev(x, zo(1), c), dev(x, zo(-1), c)
        right, left = dev(xo(1), z, c), dev(xo(-1), z, c)
        if colour == 0:
            for dx in range(1, NX):
                send(dx - 1, one(x), one(z), dev(xo(dx), z, c))
            yield
            for dx in range(1, NX):
                got(dx - 1, one(xo(-dx)), one(z))
            send(3, ALL, one(z), up)
            send(4, ALL, one(z), down)
            pass_on(42, ALL, one(z))
            for step in range(1, 4):
                yield
                got(1 + 2 * step, ALL, one(zo(-step)))
                if step < 3:
                    send(3 + 2 * step, ALL, one(zo(-step)), up)
                else:
                    send(9, pl.ds(0, 2), one(zo(-3)), up)
                got(2 + 2 * step, ALL, one(zo(step)))
                if step < 3:
                    send(4 + 2 * step, ALL, one(zo(step)), down)
                else:
                    send(10, pl.ds(2, 2), one(zo(3)), down)
                pass_on(41 + 2 * step, ALL, one(zo(-step)))
                pass_on(42 + 2 * step, ALL, one(zo(step)))
            yield
            got(9, pl.ds(0, 2), one(zo(-4)))
            got(10, pl.ds(2, 2), one(zo(4)))
            pass_on(49, ALL, one(zo(4)))
            return
        offsets = (0, -1, 1, -2, 2, -3, 3, 4)

        def sideways(j):
            at = one(zo(offsets[j]))
            send(18 + j, one(x), at, right)
            send(26 + j, one(x), at, left)

        send(11, one(x), one(z), up)
        send(12, one(x), one(z), down)
        sideways(0)
        for step in range(1, 4):
            yield
            got(9 + 2 * step, one(x), one(zo(-step)))
            if step < 3:
                send(11 + 2 * step, one(x), one(zo(-step)), up)
            elif plus:
                send(17, one(x), one(zo(-3)), up)
            sideways(2 * step - 1)
            got(10 + 2 * step, one(x), one(zo(step)))
            if step < 3:
                send(12 + 2 * step, one(x), one(zo(step)), down)
            elif not plus:
                send(17, one(x), one(zo(3)), down)
            sideways(2 * step)
        yield
        got(17, one(x), one(zo(4)))
        sideways(7)
        pass_on(50, one(x), ALL)
        for j, by in enumerate(offsets):
            yield
            got(18 + j, one(xo(-1)), one(zo(by)))
            got(26 + j, one(xo(1)), one(zo(by)))
            if j % 2 == 0:
                send(34 + j, one(xo(-1)), one(zo(by)), right)
            else:
                send(34 + j, one(xo(1)), one(zo(by)), left)
        pass_on(51, one(xo(-1)), ALL)
        pass_on(52, one(xo(1)), ALL)
        yield
        for j, by in enumerate(offsets):
            got(34 + j, one(xo(2)), one(zo(by)))
        pass_on(53, one(xo(2)), ALL)

    def follow(streams, order):
        for at in order:
            next(streams[at], None)

    pending = []
    wout[pl.ds(x, 1), pl.ds(z, 1), pl.ds(c, 1)] = wo_ref[...].reshape(1, 1, 1, 16, D)
    streams = [
        gather(tensor, colour, tensor == W_IN, pending) for tensor in (W_OUT, W_IN) for colour in (1, 0)
    ]
    follow(streams, (0, 1))
    swap = pltpu.make_async_remote_copy(
        src_ref=wi_ref, dst_ref=pair, send_sem=pair_sem.at[0], recv_sem=pair_sem.at[1],
        device_id=dev(x, z, 1 - c), device_id_type=MESH,
    )
    swap.start()

    @pl.when(seg == 0)
    def _():
        kept[pl.ds(0, SEQ), :] = queries_ref[0]
        kept[pl.ds(SEQ, SEQ), :] = passages_ref[0]

    swap.wait()
    mine, theirs = wi_ref[...].astype(F32), pair[...].astype(F32)
    both = jnp.concatenate(
        [jnp.where(c == 0, mine, theirs), jnp.where(c == 0, theirs, mine)], axis=0
    )
    half = jnp.where(c == 0, both[:, :512], both[:, 512:]).astype(BF)
    win[pl.ds(x, 1), pl.ds(z, 1), :, pl.ds(pl.multiple_of(c * 512, 512), 512)] = half.reshape(1, 1, 112, 512)
    follow(streams, WEIGHT_ORDER)
    for wait in pending:
        wait()

    def flip():
        @pl.loop(0, NX)
        def _(n):
            for j in range(8):
                part = win[n, :, :, pl.ds(128 * j, 128)].reshape(896, 128)
                win_t[pl.ds(128 * j, 128), pl.ds(pl.multiple_of(n * 896, 128), 896)] = part.T
            for j in range(7):
                part = wout[n, :, :, :, pl.ds(512 * j, 512)].reshape(256, 512)
                wout_t[pl.ds(512 * j, 512), pl.ds(pl.multiple_of(n * 256, 256), 256)] = part.T

    @pl.when(seg > 0)
    def _():
        flip()

    def hop(step, k, part, src, dst, to):
        rows = pl.ds(pl.multiple_of(k * CHUNK, CHUNK), CHUNK)
        cols = pl.ds(part * WIDE, WIDE)
        return pltpu.make_async_remote_copy(
            src_ref=src.at[rows, cols], dst_ref=dst.at[rows, cols],
            send_sem=hop_send.at[step, k, part], recv_sem=hop_recv.at[step, k, part],
            device_id=(me, to), device_id_type=MESH,
        )

    gain = gain_ref[...]
    pooled[...] = jnp.zeros_like(pooled)

    @pl.loop(0, CHUNKS)
    def _(k):
        rows = pl.ds(pl.multiple_of(k * CHUNK, CHUNK), CHUNK)

        @pl.when(seg > 0)
        def _():
            for part in range(PARTS):
                hop(0, k, part, outb, kept, seg).wait_recv()

        for part in range(CHUNK // 16):
            sub = pl.ds(pl.multiple_of(k * CHUNK + part * 16, 16), 16)
            stream = kept[sub, :].astype(F32)
            scale = lax.rsqrt(jnp.mean(stream * stream, axis=-1, keepdims=True) + EPS)
            scales[sub, :] = jnp.broadcast_to(scale, (16, 128))
            normed[pl.ds(part * 16, 16), :] = (stream * scale * gain).astype(BF)
        for n in range(KVW // 256):
            cols = pl.ds(n * 256, 256)
            v = jnp.dot(normed[...], win[:, :, :, cols].reshape(D, 256), preferred_element_type=F32)
            pre[rows, cols] = v
            act[:, cols] = gelu(v).astype(BF)
        for n in range(PARTS):
            cols = pl.ds(n * WIDE, WIDE)
            v = jnp.dot(act[...], wout[:, :, :, :, cols].reshape(KVW, WIDE), preferred_element_type=F32)
            outb[rows, cols] = (kept[rows, cols].astype(F32) + v).astype(BF)

            @pl.when(seg < NY - 1)
            def _():
                hop(0, k, n, outb, kept, seg + 1).start()

        @pl.when(seg == NY - 1)
        def _():
            half = (k * CHUNK) // SEQ
            total = jnp.zeros((8, D), F32)
            for part in range(CHUNK // 16):
                sub = pl.ds(pl.multiple_of(k * CHUNK + part * 16, 16), 16)
                scaled = outb[sub, :].astype(F32) * weight_ref[sub, 0:1]
                total = total + scaled[0:8] + scaled[8:16]
            pooled[half] += total

    @pl.when(seg == 0)
    def _():
        flip()

    @pl.when(seg == NY - 1)
    def _():
        totals, invs = [], []
        for side in range(2):
            total = jnp.sum(pooled[side], axis=0, keepdims=True)
            inv = lax.rsqrt(jnp.sum(total * total, axis=-1, keepdims=True) + EPS)
            unit = total * inv
            for k in range(PACKS):
                pack[side, k : k + 1, :] = unit[:, k * 128 : (k + 1) * 128]
            pack[side, PACKS : PACKS + 4, :] = pos_ref[0:4, :]
            emb[pl.ds(x, 1), pl.ds(z, 1), pl.ds(c, 1), pl.ds(32 * side, 32), :] = pack[side].reshape(1, 1, 1, 32, 128)
            totals.append(total)
            invs.append(inv)
        waits = []
        follow([gather(EMB, colour, True, waits) for colour in (1, 0)], EMB_ORDER)
        for wait in waits:
            wait()
        flat = emb.reshape(NQ * 64, 128)
        for k in range(PACKS):
            cols = pl.ds(k * 128, 128)
            embs[0, :, cols] = flat[pl.ds(k, NQ, stride=64), :]
            embs[1, :, cols] = flat[pl.ds(32 + k, NQ, stride=64), :]
        onehot = flat[pl.ds(PACKS, NQ, stride=64), :][:, 0:NQ]
        logits = lax.dot_general(embs[0], embs[1], NT, precision=HI, preferred_element_type=F32) / TEMP
        expo = jnp.exp(logits - jnp.max(logits, axis=1, keepdims=True))
        probs = expo / jnp.sum(expo, axis=1, keepdims=True)
        dlogits = (probs - onehot) / NQ
        ii = lax.broadcasted_iota(jnp.int32, (NQ, NQ), 0)
        jj = lax.broadcasted_iota(jnp.int32, (NQ, NQ), 1)
        row = jnp.sum(jnp.where(ii == me, dlogits, 0.0), axis=0, keepdims=True)
        col = jnp.sum(jnp.where(jj == me, dlogits, 0.0), axis=1, keepdims=True)
        row = jnp.broadcast_to(row, (8, NQ))
        dq = jnp.dot(row, embs[1], precision=HI, preferred_element_type=F32)[0:1] / TEMP
        dp = jnp.sum(col * embs[0], axis=0, keepdims=True) / TEMP
        for side, demb in enumerate((dq, dp)):
            inv, total = invs[side], totals[side]
            along = jnp.sum(total * demb, axis=-1, keepdims=True)
            grad = inv * demb - total * (inv * inv * inv) * along
            for part in range(SEQ // 16):
                sub = pl.ds(side * SEQ + part * 16, 16)
                gin[sub, :] = (weight_ref[sub, 0:1] * grad).astype(BF)

    gacc[...] = jnp.zeros_like(gacc)

    @pl.loop(0, CHUNKS)
    def _(k):
        rows = pl.ds(pl.multiple_of(k * CHUNK, CHUNK), CHUNK)

        @pl.when(seg < NY - 1)
        def _():
            for part in range(PARTS):
                hop(1, k, part, outb, gin, seg).wait_recv()
                hop(0, k, part, outb, kept, seg).wait_send()

        along = jnp.zeros((CHUNK, 1), F32)
        for n in range(KVW // 256):
            cols = pl.ds(n * 256, 256)
            back = jnp.dot(gin[rows, :], wout_t[:, cols], preferred_element_type=F32)
            v = pre[rows, cols]
            d = back * gelu_slope(v)
            along = along + jnp.sum(d * v, axis=-1, keepdims=True)
            dpre[:, cols] = d.astype(BF)
        mean = along * (1.0 / D)
        scale = scales[rows, 0:1]
        for n in range(PARTS):
            cols = pl.ds(n * WIDE, WIDE)
            dnormed = jnp.dot(dpre[...], win_t[:, cols], preferred_element_type=F32)
            unit = kept[rows, cols].astype(F32) * scale
            both = dnormed * unit
            gacc[:, cols] += both[0:8] + both[8:16] + both[16:24] + both[24:32]
            res = gin[rows, cols].astype(F32) + scale * (dnormed * gain_ref[:, cols] - unit * mean)
            outb[rows, cols] = res.astype(BF)

            @pl.when(seg > 0)
            def _():
                hop(1, k, n, outb, gin, seg - 1).start()

    qgrad_ref[...] = outb[pl.ds(0, SEQ), :].reshape(1, 1, SEQ, D)
    pgrad_ref[...] = outb[pl.ds(SEQ, SEQ), :].reshape(1, 1, SEQ, D)

    def reduce(step, buf, at, peers):
        ops = []
        for j, (target, source) in enumerate(peers):
            op = pltpu.make_async_remote_copy(
                src_ref=buf.at[at], dst_ref=buf.at[at],
                send_sem=red_send.at[step, j], recv_sem=red_recv.at[step, j],
                device_id=target, device_id_type=MESH,
            )
            op.start()
            ops.append(op.wait_send)
            ops.append(pltpu.make_async_remote_copy(
                src_ref=buf.at[source], dst_ref=buf.at[source],
                send_sem=red_send.at[step, j], recv_sem=red_recv.at[step, j],
                device_id=target, device_id_type=MESH,
            ).wait_recv)
        for op in ops:
            op()

    at = x * NC + c
    gsum = jnp.sum(gacc[...], axis=0, keepdims=True)
    for k in range(PACKS):
        pack[0, k : k + 1, :] = gsum[:, k * 128 : (k + 1) * 128]
    near[at] = pack[0]
    peers = []
    for dx in range(NX):
        for other in range(NC):
            if dx or other:
                pc = c if other == 0 else 1 - c
                peers.append((dev(xo(dx), z, pc), xo(-dx) * NC + pc))
    reduce(0, near, at, peers)
    far[z] = jnp.sum(near[...], axis=0)
    reduce(1, far, z, [(dev(x, zo(dz), c), zo(-dz)) for dz in range(1, NZ)])
    pack[1] = jnp.sum(far[...], axis=0)
    for k in range(PACKS):
        gsum_ref[0:1, k * 128 : (k + 1) * 128] = pack[1, k : k + 1, :]

    @pl.when(seg > 0)
    def _():
        for k in range(CHUNKS):
            for part in range(PARTS):
                hop(1, k, part, outb, gin, seg).wait_send()


def local(queries_in, passages_in, query_len, passage_len, positive, norm_gain, w_in, w_out):
    lengths = jnp.concatenate([query_len, passage_len])
    mask = (jnp.arange(SEQ, dtype=jnp.int32)[None, :] < lengths[:, None]).astype(F32)
    weights = mask / lengths.astype(F32)[:, None]
    weights = jnp.broadcast_to(weights.reshape(2 * SEQ, 1), (2 * SEQ, 128))
    chosen = (lax.broadcasted_iota(jnp.int32, (8, 128), 1) == positive[0]).astype(F32)
    vmem = pl.BlockSpec(memory_space=pltpu.VMEM)
    rows = 2 * SEQ
    return pl.pallas_call(
        kernel,
        out_shape=(
            jax.ShapeDtypeStruct((1, 1, SEQ, D), BF),
            jax.ShapeDtypeStruct((1, 1, SEQ, D), BF),
            jax.ShapeDtypeStruct((1, D), F32),
        ),
        in_specs=[vmem] * 7,
        out_specs=(vmem,) * 3,
        scratch_shapes=[
            pltpu.VMEM((NX, NZ, 112, KVW), BF),
            pltpu.VMEM((NX, NZ, NC, 16, D), BF),
            pltpu.VMEM((KVW, D), BF),
            pltpu.VMEM((D, KVW), BF),
            pltpu.VMEM((NX, NZ, NC, 64, 128), F32),
            pltpu.VMEM((2, NQ, D), F32),
            pltpu.VMEM((56, KVW), BF),
            pltpu.VMEM((rows, D), BF),
            pltpu.VMEM((rows, KVW), F32),
            pltpu.VMEM((rows, 128), F32),
            pltpu.VMEM((CHUNK, D), BF),
            pltpu.VMEM((CHUNK, KVW), BF),
            pltpu.VMEM((rows, D), BF),
            pltpu.VMEM((rows, D), BF),
            pltpu.VMEM((CHUNK, KVW), BF),
            pltpu.VMEM((8, D), F32),
            pltpu.VMEM((2, 8, D), F32),
            pltpu.VMEM((2, 32, 128), F32),
            pltpu.VMEM((NX * NC, 32, 128), F32),
            pltpu.VMEM((NZ, 32, 128), F32),
            pltpu.SemaphoreType.DMA((3, 54)),
            pltpu.SemaphoreType.DMA((3, 54)),
            pltpu.SemaphoreType.DMA((2,)),
            pltpu.SemaphoreType.DMA((2, CHUNKS, PARTS)),
            pltpu.SemaphoreType.DMA((2, CHUNKS, PARTS)),
            pltpu.SemaphoreType.DMA((2, 7)),
            pltpu.SemaphoreType.DMA((2, 7)),
        ],
        compiler_params=pltpu.CompilerParams(
            collective_id=0, has_side_effects=True, vmem_limit_bytes=56 * 1024 * 1024
        ),
        name="embedder_window",
    )(queries_in, passages_in, norm_gain, weights, chosen, w_in[0], w_out[0])


def solution(mesh):
    return jax.shard_map(
        local,
        mesh=mesh,
        in_specs=(
            P("dp", None, None),
            P("dp", None, None),
            P("dp"),
            P("dp"),
            P("dp"),
            P("segment", None),
            P("segment", "dp", None),
            P("segment", "dp", None),
        ),
        out_specs=(
            P("segment", "dp", None, None),
            P("segment", "dp", None, None),
            P("segment", None),
        ),
        check_vma=False,
    )
```

time: 224 us -> 189 us (0.84)
  Pallas kernels: 218 us -> 182 us
  local copies, waits for them, and re-layouts: 1.75 us -> 4.64 us
    pallas_call x1, Pallas kernels: 218 us -> 182 us  [local(): pl.pallas_call(kernel, out_shape=(jax.ShapeDtypeStruct((1, 1, SEQ, D), BF...]
    unnamed x7, local copies, waits for them, and re-layouts: 0.62 us -> 3.24 us
where the time goes in v2:
time: 189 us
  Pallas kernels  182 us (96%)
  local copies, waits for them, and re-layouts  4.64 us (2%)
  between operations  2.6 us (1%)
    pallas_call x1, Pallas kernels, local(): pl.pallas_call(kernel, out_shape=(jax.ShapeDtypeStruct((1, 1, SEQ, D), BF...  182 us

profile of v2, /device:TPU:1, one launch (start us, length us, event | category | flops | bytes accessed | tf_op | source)
XLA Modules:
  0.0 189.1 jit_solution(12839164513559033109)
XLA Ops:
  2.6 0.1 fusion.1
  2.7 0.1 fusion
  2.7 0.1 div.17
  2.8 0.6 iota.11.pos_ref
  3.4 0.7 broadcast_in_dim.2.weight_ref
  4.1 181.7 %embedder_window.1 = (bf16[1,1,64,3584]{3,2,1,0:T(8,128)(2,1)}, bf16[1,1,64,3584]{3,2,1,0:T(8,128)(2,1)}, f32[1,3584]{1,0:T(1,128)}) custom-call(bf16[1,64,3584]{2,1,0:T(8,128)(2,1)} %queries_ref.1, bf16[1,64,3584]{2,1,0:T(8,128)(2,1)} %passages_ref.1, f32[1,3584]{1,0:T(1,128)} %gain_ref.1, f32[128,128]{1,0:T(8,128)} %broadcast_in_dim.2.weight_ref, ...), custom_call_target="tpu_custom_call" | custom-call | tf_op jit(solution)/shard_map/embedder_window/pallas_call | solution.py:407
  185.8 0.0 copy-start
  185.8 1.9 copy.17
  187.7 0.0 copy-done
  187.7 0.0 copy-start.1
  187.7 0.8 copy.18
  188.5 0.0 copy-done.1
  188.5 0.6 copy.19
  (1 shorter events, 0.0 us)
Async XLA Ops:
  185.8 1.9 copy-start
  187.7 0.8 copy-start.1

commit v3 on v2

--- a/solution.py
+++ b/solution.py
@@ -21,10 +21,9 @@
 WEIGHT_ORDER = (
     2, 3, 0, 1, 2, 3, 0, 0, 1, 2, 2, 3, 2, 0, 0, 2, 0, 2, 0, 0, 1, 3, 2, 2, 2, 0, 0, 0, 2, 2, 2, 0, 1, 3, 1, 2, 0, 3,
 )
-EMB_ORDER = (0, 1, 0, 1, 1, 0, 0, 1, 0, 0, 0, 0, 0, 0, 0, 1, 0, 0, 0, 1)
 EPS = 1e-06
 C0 = math.sqrt(2.0 / math.pi)
-W_IN, W_OUT, EMB = 0, 1, 2
+EMB_Q, EMB_P, W_IN, W_OUT = 0, 1, 2, 3
 ALL = slice(None)
 NT = (((1,), (1,)), ((), ()))
 
@@ -39,11 +38,11 @@
 
 
 def kernel(
-    queries_ref, passages_ref, gain_ref, weight_ref, pos_ref, wi_ref, wo_ref,
-    qgrad_ref, pgrad_ref, gsum_ref,
+    qlen_ref, plen_ref, pos_ref, queries_ref, passages_ref, gain_ref, wi_ref, wo_ref,
+    grad_ref, gsum_ref,
     win, wout, win_t, wout_t, emb, embs, pair, kept, pre, scales, normed, act, outb, gin, dpre, gacc, pooled,
     pack, near, far,
-    ag_send, ag_recv, pair_sem, hop_send, hop_recv, red_send, red_recv,
+    ag_send, ag_recv, pair_sem, tok_sem, out_sem, hop_send, hop_recv, red_send, red_recv,
 ):
     me = lax.axis_index("dp")
     seg = lax.axis_index("segment")
@@ -73,7 +72,7 @@
         if tensor == W_OUT:
             cols = pl.ds(0, 1536) if colour == 0 else pl.ds(1536, 2048)
             return wout.at[xs, zs, pl.ds(pc, 1), :, cols]
-        return emb.at[xs, zs, pl.ds(pc, 1), pl.ds(32 * colour, 32), :]
+        return emb.at[xs, zs, pl.ds(pc, 1), pl.ds(16 * (2 * tensor + colour), 16), :]
 
     def copy_of(tensor, slot, ref, target):
         return pltpu.make_async_remote_copy(
@@ -82,6 +81,9 @@
             device_id=target, device_id_type=MESH,
         )
 
+    def one(at):
+        return pl.ds(at, 1)
+
     def gather(tensor, colour, plus, pending):
         def send(slot, xs, zs, target):
             op = copy_of(tensor, slot, piece(tensor, colour, xs, zs, c), target)
@@ -95,9 +97,6 @@
             send(slot, xs, zs, dev(x, z, 1 - c))
             other = copy_of(tensor, slot, piece(tensor, colour, xs, zs, 1 - c), dev(x, z, 1 - c))
             pending.append(other.wait_recv)
-
-        def one(at):
-            return pl.ds(at, 1)
 
         up, down = dev(x, zo(1), c), dev(x, zo(-1), c)
         right, left = dev(xo(1), z, c), dev(xo(-1), z, c)
@@ -172,6 +171,51 @@
             got(34 + j, one(xo(2)), one(zo(by)))
         pass_on(53, one(xo(2)), ALL)
 
+    def exchange(tensor):
+        def own_first():
+            ops = [(0, by - 1, one(x), one(z), dev(xo(by), z, c), one(xo(-by)), one(z)) for by in range(1, NX)]
+            return ops + [
+                (1, 2 + by, one(x), one(z), dev(x, zo(by), c), one(x), one(zo(-by))) for by in range(1, NZ)
+            ]
+
+        def along_z():
+            return [(0, 9 + by, ALL, one(z), dev(x, zo(by), c), ALL, one(zo(-by))) for by in range(1, NZ)]
+
+        def along_x():
+            return [(1, 16 + by, one(x), ALL, dev(xo(by), z, c), one(xo(-by)), ALL) for by in range(1, NX)]
+
+        def to_mate():
+            return [(colour, 20 + colour, ALL, ALL, dev(x, z, 1 - c), ALL, ALL) for colour in range(2)]
+
+        def send(ops):
+            for colour, slot, xs, zs, target, _, _ in ops:
+                copy_of(tensor, slot, piece(tensor, colour, xs, zs, c), target).start()
+
+        def got(ops, pc=c):
+            for colour, slot, _, _, target, xs, zs in ops:
+                copy_of(tensor, slot, piece(tensor, colour, xs, zs, pc), target).wait_recv()
+
+        def begin():
+            send(own_first())
+
+        def middle():
+            ops = own_first()
+            got(ops[: NX - 1])
+            send(along_z())
+            got(ops[NX - 1 :])
+            send(along_x())
+
+        def end():
+            got(along_x())
+            send(to_mate()[1:])
+            got(along_z())
+            send(to_mate()[:1])
+            got(to_mate()[::-1], 1 - c)
+            for colour, slot, xs, zs, target, _, _ in own_first() + along_z() + along_x() + to_mate():
+                copy_of(tensor, slot, piece(tensor, colour, xs, zs, c), target).wait_send()
+
+        return begin, middle, end
+
     def follow(streams, order):
         for at in order:
             next(streams[at], None)
@@ -188,10 +232,15 @@
     )
     swap.start()
 
+    tokens = [
+        pltpu.make_async_copy(ref.at[0], kept.at[pl.ds(side * SEQ, SEQ)], tok_sem.at[side])
+        for side, ref in enumerate((queries_ref, passages_ref))
+    ]
+
     @pl.when(seg == 0)
     def _():
-        kept[pl.ds(0, SEQ), :] = queries_ref[0]
-        kept[pl.ds(SEQ, SEQ), :] = passages_ref[0]
+        for op in tokens:
+            op.start()
 
     swap.wait()
     mine, theirs = wi_ref[...].astype(F32), pair[...].astype(F32)
@@ -218,6 +267,11 @@
     def _():
         flip()
 
+    @pl.when(seg == 0)
+    def _():
+        for op in tokens:
+            op.wait()
+
     def hop(step, k, part, src, dst, to):
         rows = pl.ds(pl.multiple_of(k * CHUNK, CHUNK), CHUNK)
         cols = pl.ds(part * WIDE, WIDE)
@@ -229,6 +283,27 @@
 
     gain = gain_ref[...]
     pooled[...] = jnp.zeros_like(pooled)
+
+    def weight(start, count, side):
+        length = jnp.where(side == 0, qlen_ref[0], plen_ref[0])
+        at = lax.broadcasted_iota(jnp.int32, (count, 1), 0) + start
+        return jnp.where(at < length, 1.0, 0.0) / length.astype(F32)
+
+    def norm_of(side):
+        total = jnp.sum(pooled[side], axis=0, keepdims=True)
+        return total, lax.rsqrt(jnp.sum(total * total, axis=-1, keepdims=True) + EPS)
+
+    def embed(side):
+        total, inv = norm_of(side)
+        unit = total * inv
+        for k in range(PACKS):
+            pack[side, k : k + 1, :] = unit[:, k * 128 : (k + 1) * 128]
+        spot = lax.broadcasted_iota(jnp.int32, (32 - PACKS, 128), 1)
+        pack[side, PACKS:32, :] = jnp.where(spot == pos_ref[0], 1.0, 0.0)
+        emb[pl.ds(x, 1), pl.ds(z, 1), pl.ds(c, 1), pl.ds(32 * side, 32), :] = pack[side].reshape(1, 1, 1, 32, 128)
+        return total, inv
+
+    query_steps, passage_steps = exchange(EMB_Q), exchange(EMB_P)
 
     @pl.loop(0, CHUNKS)
     def _(k):
@@ -250,9 +325,15 @@
             v = jnp.dot(normed[...], win[:, :, :, cols].reshape(D, 256), preferred_element_type=F32)
             pre[rows, cols] = v
             act[:, cols] = gelu(v).astype(BF)
+
+        def rise(n):
+            cols = pl.ds(n * WIDE, WIDE)
+            return jnp.dot(act[...], wout[:, :, :, :, cols].reshape(KVW, WIDE), preferred_element_type=F32)
+
+        ahead = rise(0)
         for n in range(PARTS):
             cols = pl.ds(n * WIDE, WIDE)
-            v = jnp.dot(act[...], wout[:, :, :, :, cols].reshape(KVW, WIDE), preferred_element_type=F32)
+            v, ahead = ahead, rise(n + 1) if n + 1 < PARTS else None
             outb[rows, cols] = (kept[rows, cols].astype(F32) + v).astype(BF)
 
             @pl.when(seg < NY - 1)
@@ -261,13 +342,22 @@
 
         @pl.when(seg == NY - 1)
         def _():
-            half = (k * CHUNK) // SEQ
+            side = (k * CHUNK) // SEQ
             total = jnp.zeros((8, D), F32)
             for part in range(CHUNK // 16):
                 sub = pl.ds(pl.multiple_of(k * CHUNK + part * 16, 16), 16)
-                scaled = outb[sub, :].astype(F32) * weight_ref[sub, 0:1]
+                scaled = outb[sub, :].astype(F32) * weight(part * 16 + (k * CHUNK) % SEQ, 16, side)
                 total = total + scaled[0:8] + scaled[8:16]
-            pooled[half] += total
+            pooled[side] += total
+
+            @pl.when(k == CHUNKS // 2 - 1)
+            def _():
+                embed(0)
+                query_steps[0]()
+
+            @pl.when(k == CHUNKS // 2)
+            def _():
+                query_steps[1]()
 
     @pl.when(seg == 0)
     def _():
@@ -275,26 +365,20 @@
 
     @pl.when(seg == NY - 1)
     def _():
-        totals, invs = [], []
-        for side in range(2):
-            total = jnp.sum(pooled[side], axis=0, keepdims=True)
-            inv = lax.rsqrt(jnp.sum(total * total, axis=-1, keepdims=True) + EPS)
-            unit = total * inv
+        flat = emb.reshape(NQ * 64, 128)
+
+        def unpack(side):
             for k in range(PACKS):
-                pack[side, k : k + 1, :] = unit[:, k * 128 : (k + 1) * 128]
-            pack[side, PACKS : PACKS + 4, :] = pos_ref[0:4, :]
-            emb[pl.ds(x, 1), pl.ds(z, 1), pl.ds(c, 1), pl.ds(32 * side, 32), :] = pack[side].reshape(1, 1, 1, 32, 128)
-            totals.append(total)
-            invs.append(inv)
-        waits = []
-        follow([gather(EMB, colour, True, waits) for colour in (1, 0)], EMB_ORDER)
-        for wait in waits:
-            wait()
-        flat = emb.reshape(NQ * 64, 128)
-        for k in range(PACKS):
-            cols = pl.ds(k * 128, 128)
-            embs[0, :, cols] = flat[pl.ds(k, NQ, stride=64), :]
-            embs[1, :, cols] = flat[pl.ds(32 + k, NQ, stride=64), :]
+                embs[side, :, pl.ds(k * 128, 128)] = flat[pl.ds(32 * side + k, NQ, stride=64), :]
+
+        passage = embed(1)
+        passage_steps[0]()
+        query_steps[2]()
+        query = norm_of(0)
+        unpack(0)
+        passage_steps[1]()
+        passage_steps[2]()
+        unpack(1)
         onehot = flat[pl.ds(PACKS, NQ, stride=64), :][:, 0:NQ]
         logits = lax.dot_general(embs[0], embs[1], NT, precision=HI, preferred_element_type=F32) / TEMP
         expo = jnp.exp(logits - jnp.max(logits, axis=1, keepdims=True))
@@ -307,13 +391,16 @@
         row = jnp.broadcast_to(row, (8, NQ))
         dq = jnp.dot(row, embs[1], precision=HI, preferred_element_type=F32)[0:1] / TEMP
         dp = jnp.sum(col * embs[0], axis=0, keepdims=True) / TEMP
-        for side, demb in enumerate((dq, dp)):
-            inv, total = invs[side], totals[side]
+        for side, (demb, (total, inv)) in enumerate(((dq, query), (dp, passage))):
             along = jnp.sum(total * demb, axis=-1, keepdims=True)
             grad = inv * demb - total * (inv * inv * inv) * along
             for part in range(SEQ // 16):
                 sub = pl.ds(side * SEQ + part * 16, 16)
-                gin[sub, :] = (weight_ref[sub, 0:1] * grad).astype(BF)
+                gin[sub, :] = (weight(part * 16, 16, side) * grad).astype(BF)
+
+    def store(k):
+        rows = pl.ds(pl.multiple_of(k * CHUNK, CHUNK), CHUNK)
+        return pltpu.make_async_copy(outb.at[rows], grad_ref.at[rows], out_sem.at[k])
 
     gacc[...] = jnp.zeros_like(gacc)
 
@@ -337,9 +424,14 @@
             dpre[:, cols] = d.astype(BF)
         mean = along * (1.0 / D)
         scale = scales[rows, 0:1]
+
+        def fall(n):
+            return jnp.dot(dpre[...], win_t[:, pl.ds(n * WIDE, WIDE)], preferred_element_type=F32)
+
+        ahead = fall(0)
         for n in range(PARTS):
             cols = pl.ds(n * WIDE, WIDE)
-            dnormed = jnp.dot(dpre[...], win_t[:, cols], preferred_element_type=F32)
+            dnormed, ahead = ahead, fall(n + 1) if n + 1 < PARTS else None
             unit = kept[rows, cols].astype(F32) * scale
             both = dnormed * unit
             gacc[:, cols] += both[0:8] + both[8:16] + both[16:24] + both[24:32]
@@ -350,8 +442,7 @@
             def _():
                 hop(1, k, n, outb, gin, seg - 1).start()
 
-    qgrad_ref[...] = outb[pl.ds(0, SEQ), :].reshape(1, 1, SEQ, D)
-    pgrad_ref[...] = outb[pl.ds(SEQ, SEQ), :].reshape(1, 1, SEQ, D)
+        store(k).start()
 
     def reduce(step, buf, at, peers):
         ops = []
@@ -385,9 +476,9 @@
     reduce(0, near, at, peers)
     far[z] = jnp.sum(near[...], axis=0)
     reduce(1, far, z, [(dev(x, zo(dz), c), zo(-dz)) for dz in range(1, NZ)])
-    pack[1] = jnp.sum(far[...], axis=0)
-    for k in range(PACKS):
-        gsum_ref[0:1, k * 128 : (k + 1) * 128] = pack[1, k : k + 1, :]
+    gsum_ref[...] = jnp.sum(far[...], axis=0)
+    for k in range(CHUNKS):
+        store(k).wait()
 
     @pl.when(seg > 0)
     def _():
@@ -397,22 +488,17 @@
 
 
 def local(queries_in, passages_in, query_len, passage_len, positive, norm_gain, w_in, w_out):
-    lengths = jnp.concatenate([query_len, passage_len])
-    mask = (jnp.arange(SEQ, dtype=jnp.int32)[None, :] < lengths[:, None]).astype(F32)
-    weights = mask / lengths.astype(F32)[:, None]
-    weights = jnp.broadcast_to(weights.reshape(2 * SEQ, 1), (2 * SEQ, 128))
-    chosen = (lax.broadcasted_iota(jnp.int32, (8, 128), 1) == positive[0]).astype(F32)
-    vmem = pl.BlockSpec(memory_space=pltpu.VMEM)
+    vmem, hbm = pl.BlockSpec(memory_space=pltpu.VMEM), pl.BlockSpec(memory_space=pl.ANY)
+    smem = pl.BlockSpec(memory_space=pltpu.SMEM)
     rows = 2 * SEQ
-    return pl.pallas_call(
+    grads, gains = pl.pallas_call(
         kernel,
         out_shape=(
-            jax.ShapeDtypeStruct((1, 1, SEQ, D), BF),
-            jax.ShapeDtypeStruct((1, 1, SEQ, D), BF),
-            jax.ShapeDtypeStruct((1, D), F32),
+            jax.ShapeDtypeStruct((rows, D), BF),
+            jax.ShapeDtypeStruct((32, 128), F32),
         ),
-        in_specs=[vmem] * 7,
-        out_specs=(vmem,) * 3,
+        in_specs=[smem] * 3 + [hbm] * 2 + [vmem] * 3,
+        out_specs=(hbm, vmem),
         scratch_shapes=[
             pltpu.VMEM((NX, NZ, 112, KVW), BF),
             pltpu.VMEM((NX, NZ, NC, 16, D), BF),
@@ -434,9 +520,11 @@
             pltpu.VMEM((2, 32, 128), F32),
             pltpu.VMEM((NX * NC, 32, 128), F32),
             pltpu.VMEM((NZ, 32, 128), F32),
-            pltpu.SemaphoreType.DMA((3, 54)),
-            pltpu.SemaphoreType.DMA((3, 54)),
+            pltpu.SemaphoreType.DMA((4, 54)),
+            pltpu.SemaphoreType.DMA((4, 54)),
             pltpu.SemaphoreType.DMA((2,)),
+            pltpu.SemaphoreType.DMA((2,)),
+            pltpu.SemaphoreType.DMA((CHUNKS,)),
             pltpu.SemaphoreType.DMA((2, CHUNKS, PARTS)),
             pltpu.SemaphoreType.DMA((2, CHUNKS, PARTS)),
             pltpu.SemaphoreType.DMA((2, 7)),
@@ -446,7 +534,9 @@
             collective_id=0, has_side_effects=True, vmem_limit_bytes=56 * 1024 * 1024
         ),
         name="embedder_window",
-    )(queries_in, passages_in, norm_gain, weights, chosen, w_in[0], w_out[0])
+    )(query_len, passage_len, positive, queries_in, passages_in, norm_gain, w_in[0], w_out[0])
+    grads = grads.reshape(2, 1, 1, SEQ, D)
+    return grads[0], grads[1], gains[:PACKS].reshape(1, D)
 
 
 def solution(mesh):

time: 189 us -> 181 us (0.958)
  Pallas kernels: 182 us -> 175 us
    pallas_call x1, Pallas kernels: 182 us -> 175 us  [local(): pl.pallas_call(kernel, out_shape=(jax.ShapeDtypeStruct((rows, D), BF), ja...]
    unnamed x7 -> x4, local copies, waits for them, and re-layouts: 3.24 us -> 0.62 us
    squeeze x0 -> x1, local copies, waits for them, and re-layouts: none -> 2.14 us  [local(): return (grads[0], grads[1], gains[:PACKS].reshape(1, D))]
where the time goes in v3:
time: 181 us
  Pallas kernels  175 us (97%)
  local copies, waits for them, and re-layouts  2.76 us (2%)
  between operations  2.59 us (1%)
    pallas_call x1, Pallas kernels, local(): pl.pallas_call(kernel, out_shape=(jax.ShapeDtypeStruct((rows, D), BF), ja...  175 us

profile of v3, /device:TPU:1, one launch (start us, length us, event | category | flops | bytes accessed | tf_op | source)
XLA Modules:
  0.0 180.8 jit_solution(4395610180127642845)
XLA Ops:
  2.6 175.4 %embedder_window.1 = (bf16[128,3584]{1,0:T(8,128)(2,1)}, f32[32,128]{1,0:T(8,128)}) custom-call(s32[1]{0:T(128)S(6)} %copy.14.qlen_ref, s32[1]{0:T(128)S(6)} %copy.15.plen_ref, s32[1]{0:T(128)S(6)} %copy.16.pos_ref, bf16[1,64,3584]{2,1,0:T(8,128)(2,1)} %queries_ref.1, bf16[1,64,3584]{2,1,0:T(8,128)(2,1)} %passages_ref.1, f32[1,3584]{1,0:T(1,128)} %gain_ref.1, ...), custom_call_target="tpu_custom_call" | custom-call | tf_op jit(solution)/shard_map/embedder_window/pallas_call | solution.py:494
  178.0 0.0 copy-start
  178.0 2.1 %slice_bitcast_fusion = (bf16[1,1,64,3584]{3,2,1,0:T(8,128)(2,1)}, bf16[1,1,64,3584]{3,2,1,0:T(8,128)(2,1)}) fusion(bf16[128,3584]{1,0:T(8,128)(2,1)} %get-tuple-element.5), kind=kLoop, calls=%fused_computation | loop fusion | bytes 1835008 | tf_op jit(solution)/shard_map/squeeze | solution.py:539
  180.1 0.0 copy-done
  180.2 0.6 copy.13
  (1 shorter events, 0.0 us)
Async XLA Ops:
  178.0 2.2 %copy-start = (f32[32,128]{1,0:T(8,128)S(1)}, f32[32,128]{1,0:T(8,128)}, u32[]{:S(2)}) copy-start(f32[32,128]{1,0:T(8,128)} %get-tuple-element.6) | copy-start | bytes 49156

commit v4 on v3

--- a/solution.py
+++ b/solution.py
@@ -18,8 +18,9 @@
 PARTS = 4
 WIDE = D // PARTS
 PACKS = D // 128
+FAR_X, FAR_Z = (2, 1, 3), (4, 3, 5, 2, 6, 1, 7)
 WEIGHT_ORDER = (
-    2, 3, 0, 1, 2, 3, 0, 0, 1, 2, 2, 3, 2, 0, 0, 2, 0, 2, 0, 0, 1, 3, 2, 2, 2, 0, 0, 0, 2, 2, 2, 0, 1, 3, 1, 2, 0, 3,
+    2, 3, 0, 1, 2, 3, 0, 1, 2, 2, 0, 3, 2, 0, 0, 0, 2, 0, 2, 1, 0, 3, 2, 2, 0, 2, 2, 0, 0, 0, 1, 2, 2, 3, 2, 0, 1, 3,
 )
 EPS = 1e-06
 C0 = math.sqrt(2.0 / math.pi)
@@ -38,11 +39,11 @@
 
 
 def kernel(
-    qlen_ref, plen_ref, pos_ref, queries_ref, passages_ref, gain_ref, wi_ref, wo_ref,
+    qlen_ref, plen_ref, pos_ref, queries_ref, passages_ref, gain_hbm, wi_hbm, wo_hbm,
     grad_ref, gsum_ref,
-    win, wout, win_t, wout_t, emb, embs, pair, kept, pre, scales, normed, act, outb, gin, dpre, gacc, pooled,
+    win, wout, win_t, wout_t, emb, embs, gain_ref, wi_ref, pair, kept, pre, scales, act, outb, gin, dpre, gacc, pooled,
     pack, near, far,
-    ag_send, ag_recv, pair_sem, tok_sem, out_sem, hop_send, hop_recv, red_send, red_recv,
+    ag_send, ag_recv, pair_sem, tok_sem, hop_send, hop_recv, red_send, red_recv,
 ):
     me = lax.axis_index("dp")
     seg = lax.axis_index("segment")
@@ -56,6 +57,22 @@
 
     def zo(by):
         return (z + by + NZ) % NZ
+
+    own = [
+        pltpu.make_async_copy(src, dst, tok_sem.at[2 + j])
+        for j, (src, dst) in enumerate(((wo_hbm, wout.at[x, z, c]), (wi_hbm, wi_ref), (gain_hbm, gain_ref)))
+    ]
+    for op in own:
+        op.start()
+    tokens = [
+        pltpu.make_async_copy(ref.at[0], kept.at[pl.ds(side * SEQ, SEQ)], tok_sem.at[side])
+        for side, ref in enumerate((queries_ref, passages_ref))
+    ]
+
+    @pl.when(seg == 0)
+    def _():
+        for op in tokens:
+            op.start()
 
     barrier = pltpu.get_barrier_semaphore()
     mates = [dev(xo(dx), z, pc) for dx in range(NX) for pc in (c, 1 - c)][1:]
@@ -72,7 +89,8 @@
         if tensor == W_OUT:
             cols = pl.ds(0, 1536) if colour == 0 else pl.ds(1536, 2048)
             return wout.at[xs, zs, pl.ds(pc, 1), :, cols]
-        return emb.at[xs, zs, pl.ds(pc, 1), pl.ds(16 * (2 * tensor + colour), 16), :]
+        rows = pl.ds(32 * tensor, 8) if colour == 0 else pl.ds(32 * tensor + 8, 24)
+        return emb.at[xs, zs, pl.ds(pc, 1), rows, :]
 
     def copy_of(tensor, slot, ref, target):
         return pltpu.make_async_remote_copy(
@@ -84,11 +102,11 @@
     def one(at):
         return pl.ds(at, 1)
 
-    def gather(tensor, colour, plus, pending):
+    def gather(tensor, colour, plus):
         def send(slot, xs, zs, target):
             op = copy_of(tensor, slot, piece(tensor, colour, xs, zs, c), target)
             op.start()
-            pending.append(op.wait_send)
+            unsent.append(op.wait_send)
 
         def got(slot, xs, zs):
             copy_of(tensor, slot, piece(tensor, colour, xs, zs, c), dev(x, z, 1 - c)).wait_recv()
@@ -173,16 +191,14 @@
 
     def exchange(tensor):
         def own_first():
-            ops = [(0, by - 1, one(x), one(z), dev(xo(by), z, c), one(xo(-by)), one(z)) for by in range(1, NX)]
-            return ops + [
-                (1, 2 + by, one(x), one(z), dev(x, zo(by), c), one(x), one(zo(-by))) for by in range(1, NZ)
-            ]
+            ops = [(0, by - 1, one(x), one(z), dev(xo(by), z, c), one(xo(-by)), one(z)) for by in FAR_X]
+            return ops + [(1, 2 + by, one(x), one(z), dev(x, zo(by), c), one(x), one(zo(-by))) for by in FAR_Z]
 
         def along_z():
-            return [(0, 9 + by, ALL, one(z), dev(x, zo(by), c), ALL, one(zo(-by))) for by in range(1, NZ)]
+            return [(0, 9 + by, ALL, one(z), dev(x, zo(by), c), ALL, one(zo(-by))) for by in FAR_Z]
 
         def along_x():
-            return [(1, 16 + by, one(x), ALL, dev(xo(by), z, c), one(xo(-by)), ALL) for by in range(1, NX)]
+            return [(1, 16 + by, one(x), ALL, dev(xo(by), z, c), one(xo(-by)), ALL) for by in FAR_X]
 
         def to_mate():
             return [(colour, 20 + colour, ALL, ALL, dev(x, z, 1 - c), ALL, ALL) for colour in range(2)]
@@ -220,10 +236,11 @@
         for at in order:
             next(streams[at], None)
 
-    pending = []
-    wout[pl.ds(x, 1), pl.ds(z, 1), pl.ds(c, 1)] = wo_ref[...].reshape(1, 1, 1, 16, D)
+    pending, unsent = [], []
+    for op in own:
+        op.wait()
     streams = [
-        gather(tensor, colour, tensor == W_IN, pending) for tensor in (W_OUT, W_IN) for colour in (1, 0)
+        gather(tensor, colour, tensor == W_IN) for tensor in (W_OUT, W_IN) for colour in (1, 0)
     ]
     follow(streams, (0, 1))
     swap = pltpu.make_async_remote_copy(
@@ -231,16 +248,6 @@
         device_id=dev(x, z, 1 - c), device_id_type=MESH,
     )
     swap.start()
-
-    tokens = [
-        pltpu.make_async_copy(ref.at[0], kept.at[pl.ds(side * SEQ, SEQ)], tok_sem.at[side])
-        for side, ref in enumerate((queries_ref, passages_ref))
-    ]
-
-    @pl.when(seg == 0)
-    def _():
-        for op in tokens:
-            op.start()
 
     swap.wait()
     mine, theirs = wi_ref[...].astype(F32), pair[...].astype(F32)
@@ -266,6 +273,8 @@
     @pl.when(seg > 0)
     def _():
         flip()
+        for wait in unsent:
+            wait()
 
     @pl.when(seg == 0)
     def _():
@@ -281,7 +290,6 @@
             device_id=(me, to), device_id_type=MESH,
         )
 
-    gain = gain_ref[...]
     pooled[...] = jnp.zeros_like(pooled)
 
     def weight(start, count, side):
@@ -309,22 +317,24 @@
     def _(k):
         rows = pl.ds(pl.multiple_of(k * CHUNK, CHUNK), CHUNK)
 
-        @pl.when(seg > 0)
-        def _():
-            for part in range(PARTS):
-                hop(0, k, part, outb, kept, seg).wait_recv()
-
-        for part in range(CHUNK // 16):
-            sub = pl.ds(pl.multiple_of(k * CHUNK + part * 16, 16), 16)
-            stream = kept[sub, :].astype(F32)
-            scale = lax.rsqrt(jnp.mean(stream * stream, axis=-1, keepdims=True) + EPS)
-            scales[sub, :] = jnp.broadcast_to(scale, (16, 128))
-            normed[pl.ds(part * 16, 16), :] = (stream * scale * gain).astype(BF)
-        for n in range(KVW // 256):
-            cols = pl.ds(n * 256, 256)
-            v = jnp.dot(normed[...], win[:, :, :, cols].reshape(D, 256), preferred_element_type=F32)
-            pre[rows, cols] = v
-            act[:, cols] = gelu(v).astype(BF)
+        square = jnp.zeros((CHUNK, 1), F32)
+        v = jnp.zeros((CHUNK, KVW), F32)
+        for n in range(PARTS):
+            cols = pl.ds(n * WIDE, WIDE)
+
+            @pl.when(seg > 0)
+            def _():
+                hop(0, k, n, outb, kept, seg).wait_recv()
+
+            stream = kept[rows, cols].astype(F32)
+            square = square + jnp.sum(stream * stream, axis=-1, keepdims=True)
+            gained = (stream * gain_ref[:, cols]).astype(BF)
+            v = v + jnp.dot(gained, win[n].reshape(WIDE, KVW), preferred_element_type=F32)
+        scale = lax.rsqrt(square * (1.0 / D) + EPS)
+        scales[rows, :] = jnp.broadcast_to(scale, (CHUNK, 128))
+        v = v * scale
+        pre[rows, :] = v
+        act[...] = gelu(v).astype(BF)
 
         def rise(n):
             cols = pl.ds(n * WIDE, WIDE)
@@ -362,6 +372,8 @@
     @pl.when(seg == 0)
     def _():
         flip()
+        for wait in unsent:
+            wait()
 
     @pl.when(seg == NY - 1)
     def _():
@@ -398,30 +410,25 @@
                 sub = pl.ds(side * SEQ + part * 16, 16)
                 gin[sub, :] = (weight(part * 16, 16, side) * grad).astype(BF)
 
-    def store(k):
-        rows = pl.ds(pl.multiple_of(k * CHUNK, CHUNK), CHUNK)
-        return pltpu.make_async_copy(outb.at[rows], grad_ref.at[rows], out_sem.at[k])
-
     gacc[...] = jnp.zeros_like(gacc)
 
     @pl.loop(0, CHUNKS)
     def _(k):
         rows = pl.ds(pl.multiple_of(k * CHUNK, CHUNK), CHUNK)
 
-        @pl.when(seg < NY - 1)
-        def _():
-            for part in range(PARTS):
-                hop(1, k, part, outb, gin, seg).wait_recv()
-                hop(0, k, part, outb, kept, seg).wait_send()
-
-        along = jnp.zeros((CHUNK, 1), F32)
-        for n in range(KVW // 256):
-            cols = pl.ds(n * 256, 256)
-            back = jnp.dot(gin[rows, :], wout_t[:, cols], preferred_element_type=F32)
-            v = pre[rows, cols]
-            d = back * gelu_slope(v)
-            along = along + jnp.sum(d * v, axis=-1, keepdims=True)
-            dpre[:, cols] = d.astype(BF)
+        back = jnp.zeros((CHUNK, KVW), F32)
+        for n in range(PARTS):
+            cols = pl.ds(n * WIDE, WIDE)
+
+            @pl.when(seg < NY - 1)
+            def _():
+                hop(1, k, n, grad_ref, gin, seg).wait_recv()
+
+            back = back + jnp.dot(gin[rows, cols], wout_t[cols, :], preferred_element_type=F32)
+        v = pre[rows, :]
+        d = back * gelu_slope(v)
+        along = jnp.sum(d * v, axis=-1, keepdims=True)
+        dpre[...] = d.astype(BF)
         mean = along * (1.0 / D)
         scale = scales[rows, 0:1]
 
@@ -436,16 +443,14 @@
             both = dnormed * unit
             gacc[:, cols] += both[0:8] + both[8:16] + both[16:24] + both[24:32]
             res = gin[rows, cols].astype(F32) + scale * (dnormed * gain_ref[:, cols] - unit * mean)
-            outb[rows, cols] = res.astype(BF)
+            grad_ref[rows, cols] = res.astype(BF)
 
             @pl.when(seg > 0)
             def _():
-                hop(1, k, n, outb, gin, seg - 1).start()
-
-        store(k).start()
+                hop(1, k, n, grad_ref, gin, seg - 1).start()
 
     def reduce(step, buf, at, peers):
-        ops = []
+        ops, sent = [], []
         for j, (target, source) in enumerate(peers):
             op = pltpu.make_async_remote_copy(
                 src_ref=buf.at[at], dst_ref=buf.at[at],
@@ -453,7 +458,7 @@
                 device_id=target, device_id_type=MESH,
             )
             op.start()
-            ops.append(op.wait_send)
+            sent.append(op.wait_send)
             ops.append(pltpu.make_async_remote_copy(
                 src_ref=buf.at[source], dst_ref=buf.at[source],
                 send_sem=red_send.at[step, j], recv_sem=red_recv.at[step, j],
@@ -461,6 +466,7 @@
             ).wait_recv)
         for op in ops:
             op()
+        return sent
 
     at = x * NC + c
     gsum = jnp.sum(gacc[...], axis=0, keepdims=True)
@@ -468,27 +474,31 @@
         pack[0, k : k + 1, :] = gsum[:, k * 128 : (k + 1) * 128]
     near[at] = pack[0]
     peers = []
-    for dx in range(NX):
-        for other in range(NC):
-            if dx or other:
-                pc = c if other == 0 else 1 - c
-                peers.append((dev(xo(dx), z, pc), xo(-dx) * NC + pc))
-    reduce(0, near, at, peers)
+    for dx in FAR_X + (0,):
+        for pc in (c, 1 - c) if dx else (1 - c,):
+            peers.append((dev(xo(dx), z, pc), xo(-dx) * NC + pc))
+    sent = reduce(0, near, at, peers)
     far[z] = jnp.sum(near[...], axis=0)
-    reduce(1, far, z, [(dev(x, zo(dz), c), zo(-dz)) for dz in range(1, NZ)])
+    sent += reduce(1, far, z, [(dev(x, zo(dz), c), zo(-dz)) for dz in FAR_Z])
     gsum_ref[...] = jnp.sum(far[...], axis=0)
-    for k in range(CHUNKS):
-        store(k).wait()
+    for op in sent:
+        op()
 
     @pl.when(seg > 0)
     def _():
         for k in range(CHUNKS):
             for part in range(PARTS):
-                hop(1, k, part, outb, gin, seg).wait_send()
+                hop(1, k, part, grad_ref, gin, seg).wait_send()
+
+    @pl.when(seg < NY - 1)
+    def _():
+        for k in range(CHUNKS):
+            for part in range(PARTS):
+                hop(0, k, part, outb, kept, seg).wait_send()
 
 
 def local(queries_in, passages_in, query_len, passage_len, positive, norm_gain, w_in, w_out):
-    vmem, hbm = pl.BlockSpec(memory_space=pltpu.VMEM), pl.BlockSpec(memory_space=pl.ANY)
+    vmem, hbm = pl.BlockSpec(memory_space=pltpu.VMEM), pl.BlockSpec(memory_space=pltpu.HBM)
     smem = pl.BlockSpec(memory_space=pltpu.SMEM)
     rows = 2 * SEQ
     grads, gains = pl.pallas_call(
@@ -497,8 +507,8 @@
             jax.ShapeDtypeStruct((rows, D), BF),
             jax.ShapeDtypeStruct((32, 128), F32),
         ),
-        in_specs=[smem] * 3 + [hbm] * 2 + [vmem] * 3,
-        out_specs=(hbm, vmem),
+        in_specs=[smem] * 3 + [hbm] * 5,
+        out_specs=(vmem, vmem),
         scratch_shapes=[
             pltpu.VMEM((NX, NZ, 112, KVW), BF),
             pltpu.VMEM((NX, NZ, NC, 16, D), BF),
@@ -506,11 +516,12 @@
             pltpu.VMEM((D, KVW), BF),
             pltpu.VMEM((NX, NZ, NC, 64, 128), F32),
             pltpu.VMEM((2, NQ, D), F32),
+            pltpu.VMEM((1, D), F32),
+            pltpu.VMEM((56, KVW), BF),
             pltpu.VMEM((56, KVW), BF),
             pltpu.VMEM((rows, D), BF),
             pltpu.VMEM((rows, KVW), F32),
             pltpu.VMEM((rows, 128), F32),
-            pltpu.VMEM((CHUNK, D), BF),
             pltpu.VMEM((CHUNK, KVW), BF),
             pltpu.VMEM((rows, D), BF),
             pltpu.VMEM((rows, D), BF),
@@ -523,15 +534,14 @@
             pltpu.SemaphoreType.DMA((4, 54)),
             pltpu.SemaphoreType.DMA((4, 54)),
             pltpu.SemaphoreType.DMA((2,)),
-            pltpu.SemaphoreType.DMA((2,)),
-            pltpu.SemaphoreType.DMA((CHUNKS,)),
+            pltpu.SemaphoreType.DMA((5,)),
             pltpu.SemaphoreType.DMA((2, CHUNKS, PARTS)),
             pltpu.SemaphoreType.DMA((2, CHUNKS, PARTS)),
             pltpu.SemaphoreType.DMA((2, 7)),
             pltpu.SemaphoreType.DMA((2, 7)),
         ],
         compiler_params=pltpu.CompilerParams(
-            collective_id=0, has_side_effects=True, vmem_limit_bytes=56 * 1024 * 1024
+            collective_id=0, has_side_effects=True, vmem_limit_bytes=58 * 1024 * 1024
         ),
         name="embedder_window",
     )(query_len, passage_len, positive, queries_in, passages_in, norm_gain, w_in[0], w_out[0])

time: 181 us -> 172 us (0.950)
  Pallas kernels: 175 us -> 166 us
    pallas_call x1, Pallas kernels: 175 us -> 166 us  [local(): pl.pallas_call(kernel, out_shape=(jax.ShapeDtypeStruct((rows, D), BF), ja...]
where the time goes in v4:
time: 172 us
  Pallas kernels  166 us (97%)
  local copies, waits for them, and re-layouts  2.76 us (2%)
  between operations  2.59 us (2%)
    pallas_call x1, Pallas kernels, local(): pl.pallas_call(kernel, out_shape=(jax.ShapeDtypeStruct((rows, D), BF), ja...  166 us

profile of v4, /device:TPU:1, one launch (start us, length us, event | category | flops | bytes accessed | tf_op | source)
XLA Modules:
  0.0 171.5 jit_solution(53710640650379132)
XLA Ops:
  2.6 166.2 %embedder_window.1 = (bf16[128,3584]{1,0:T(8,128)(2,1)}, f32[32,128]{1,0:T(8,128)}) custom-call(s32[1]{0:T(128)S(6)} %copy.14.qlen_ref, s32[1]{0:T(128)S(6)} %copy.15.plen_ref, s32[1]{0:T(128)S(6)} %copy.16.pos_ref, bf16[1,64,3584]{2,1,0:T(8,128)(2,1)} %queries_ref.1, bf16[1,64,3584]{2,1,0:T(8,128)(2,1)} %passages_ref.1, f32[1,3584]{1,0:T(1,128)} %gain_hbm.1, ...), custom_call_target="tpu_custom_call" | custom-call | tf_op jit(solution)/shard_map/embedder_window/pallas_call | solution.py:504
  168.7 0.0 copy-start
  168.7 2.1 %slice_bitcast_fusion = (bf16[1,1,64,3584]{3,2,1,0:T(8,128)(2,1)}, bf16[1,1,64,3584]{3,2,1,0:T(8,128)(2,1)}) fusion(bf16[128,3584]{1,0:T(8,128)(2,1)} %get-tuple-element.5), kind=kLoop, calls=%fused_computation | loop fusion | bytes 1835008 | tf_op jit(solution)/shard_map/squeeze | solution.py:549
  170.9 0.0 copy-done
  170.9 0.6 copy.13
  (1 shorter events, 0.0 us)
Async XLA Ops:
  168.7 2.2 %copy-start = (f32[32,128]{1,0:T(8,128)S(1)}, f32[32,128]{1,0:T(8,128)}, u32[]{:S(2)}) copy-start(f32[32,128]{1,0:T(8,128)} %get-tuple-element.6) | copy-start | bytes 49156

commit v5 on v4

--- a/solution.py
+++ b/solution.py
@@ -24,7 +24,7 @@
 )
 EPS = 1e-06
 C0 = math.sqrt(2.0 / math.pi)
-EMB_Q, EMB_P, W_IN, W_OUT = 0, 1, 2, 3
+EMB_P, EMB_Q, W_IN, W_OUT = 0, 1, 2, 3
 ALL = slice(None)
 NT = (((1,), (1,)), ((), ()))
 
@@ -66,7 +66,7 @@
         op.start()
     tokens = [
         pltpu.make_async_copy(ref.at[0], kept.at[pl.ds(side * SEQ, SEQ)], tok_sem.at[side])
-        for side, ref in enumerate((queries_ref, passages_ref))
+        for side, ref in enumerate((passages_ref, queries_ref))
     ]
 
     @pl.when(seg == 0)
@@ -293,7 +293,7 @@
     pooled[...] = jnp.zeros_like(pooled)
 
     def weight(start, count, side):
-        length = jnp.where(side == 0, qlen_ref[0], plen_ref[0])
+        length = jnp.where(side == 0, plen_ref[0], qlen_ref[0])
         at = lax.broadcasted_iota(jnp.int32, (count, 1), 0) + start
         return jnp.where(at < length, 1.0, 0.0) / length.astype(F32)
 
@@ -309,7 +309,7 @@
         spot = lax.broadcasted_iota(jnp.int32, (32 - PACKS, 128), 1)
         pack[side, PACKS:32, :] = jnp.where(spot == pos_ref[0], 1.0, 0.0)
         emb[pl.ds(x, 1), pl.ds(z, 1), pl.ds(c, 1), pl.ds(32 * side, 32), :] = pack[side].reshape(1, 1, 1, 32, 128)
-        return total, inv
+        return unit
 
     query_steps, passage_steps = exchange(EMB_Q), exchange(EMB_P)
 
@@ -363,11 +363,11 @@
             @pl.when(k == CHUNKS // 2 - 1)
             def _():
                 embed(0)
-                query_steps[0]()
+                passage_steps[0]()
 
             @pl.when(k == CHUNKS // 2)
             def _():
-                query_steps[1]()
+                passage_steps[1]()
 
     @pl.when(seg == 0)
     def _():
@@ -375,45 +375,50 @@
         for wait in unsent:
             wait()
 
+    flat = emb.reshape(NQ * 64, 128)
+
+    def unpack(side):
+        for k in range(PACKS):
+            embs[side, :, pl.ds(k * 128, 128)] = flat[pl.ds(32 * side + k, NQ, stride=64), :]
+
+    def excess(logits, onehot):
+        expo = jnp.exp(logits - jnp.max(logits, axis=1, keepdims=True))
+        return (expo / jnp.sum(expo, axis=1, keepdims=True) - onehot) / NQ
+
+    def spread_back(side, demb):
+        total, inv = norm_of(side)
+        along = jnp.sum(total * demb, axis=-1, keepdims=True)
+        grad = inv * demb - total * (inv * inv * inv) * along
+        for part in range(SEQ // 16):
+            sub = pl.ds(side * SEQ + part * 16, 16)
+            gin[sub, :] = (weight(part * 16, 16, side) * grad).astype(BF)
+
     @pl.when(seg == NY - 1)
     def _():
-        flat = emb.reshape(NQ * 64, 128)
-
-        def unpack(side):
-            for k in range(PACKS):
-                embs[side, :, pl.ds(k * 128, 128)] = flat[pl.ds(32 * side + k, NQ, stride=64), :]
-
-        passage = embed(1)
-        passage_steps[0]()
-        query_steps[2]()
-        query = norm_of(0)
+        unit = embed(1)
+        query_steps[0]()
+        passage_steps[2]()
         unpack(0)
-        passage_steps[1]()
-        passage_steps[2]()
+        unit = jnp.broadcast_to(unit, (8, D))
+        logits = lax.dot_general(unit, embs[0], NT, precision=HI, preferred_element_type=F32) / TEMP
+        spot = lax.broadcasted_iota(jnp.int32, (8, NQ), 1)
+        dlogits = excess(logits, jnp.where(spot == pos_ref[0], 1.0, 0.0))
+        spread_back(1, jnp.dot(dlogits, embs[0], precision=HI, preferred_element_type=F32)[0:1] / TEMP)
+
+    def passages_back():
         unpack(1)
         onehot = flat[pl.ds(PACKS, NQ, stride=64), :][:, 0:NQ]
-        logits = lax.dot_general(embs[0], embs[1], NT, precision=HI, preferred_element_type=F32) / TEMP
-        expo = jnp.exp(logits - jnp.max(logits, axis=1, keepdims=True))
-        probs = expo / jnp.sum(expo, axis=1, keepdims=True)
-        dlogits = (probs - onehot) / NQ
-        ii = lax.broadcasted_iota(jnp.int32, (NQ, NQ), 0)
+        logits = lax.dot_general(embs[1], embs[0], NT, precision=HI, preferred_element_type=F32) / TEMP
+        dlogits = excess(logits, onehot)
         jj = lax.broadcasted_iota(jnp.int32, (NQ, NQ), 1)
-        row = jnp.sum(jnp.where(ii == me, dlogits, 0.0), axis=0, keepdims=True)
         col = jnp.sum(jnp.where(jj == me, dlogits, 0.0), axis=1, keepdims=True)
-        row = jnp.broadcast_to(row, (8, NQ))
-        dq = jnp.dot(row, embs[1], precision=HI, preferred_element_type=F32)[0:1] / TEMP
-        dp = jnp.sum(col * embs[0], axis=0, keepdims=True) / TEMP
-        for side, (demb, (total, inv)) in enumerate(((dq, query), (dp, passage))):
-            along = jnp.sum(total * demb, axis=-1, keepdims=True)
-            grad = inv * demb - total * (inv * inv * inv) * along
-            for part in range(SEQ // 16):
-                sub = pl.ds(side * SEQ + part * 16, 16)
-                gin[sub, :] = (weight(part * 16, 16, side) * grad).astype(BF)
+        spread_back(0, jnp.sum(col * embs[1], axis=0, keepdims=True) / TEMP)
 
     gacc[...] = jnp.zeros_like(gacc)
 
     @pl.loop(0, CHUNKS)
-    def _(k):
+    def _(step):
+        k = CHUNKS - 1 - step
         rows = pl.ds(pl.multiple_of(k * CHUNK, CHUNK), CHUNK)
 
         back = jnp.zeros((CHUNK, KVW), F32)
@@ -448,6 +453,15 @@
             @pl.when(seg > 0)
             def _():
                 hop(1, k, n, grad_ref, gin, seg - 1).start()
+
+        @pl.when((seg == NY - 1) & (step == 0))
+        def _():
+            query_steps[1]()
+
+        @pl.when((seg == NY - 1) & (step == CHUNKS // 2 - 1))
+        def _():
+            query_steps[2]()
+            passages_back()
 
     def reduce(step, buf, at, peers):
         ops, sent = [], []
@@ -546,7 +560,7 @@
         name="embedder_window",
     )(query_len, passage_len, positive, queries_in, passages_in, norm_gain, w_in[0], w_out[0])
     grads = grads.reshape(2, 1, 1, SEQ, D)
-    return grads[0], grads[1], gains[:PACKS].reshape(1, D)
+    return grads[1], grads[0], gains[:PACKS].reshape(1, D)
 
 
 def solution(mesh):

time: 172 us -> 163 us (0.948)
  Pallas kernels: 166 us -> 158 us
    pallas_call x1, Pallas kernels: 166 us -> 158 us  [local(): pl.pallas_call(kernel, out_shape=(jax.ShapeDtypeStruct((rows, D), BF), ja...]
where the time goes in v5:
time: 163 us
  Pallas kernels  158 us (97%)
  local copies, waits for them, and re-layouts  2.76 us (2%)
  between operations  2.59 us (2%)
    pallas_call x1, Pallas kernels, local(): pl.pallas_call(kernel, out_shape=(jax.ShapeDtypeStruct((rows, D), BF), ja...  158 us

profile of v5, /device:TPU:1, one launch (start us, length us, event | category | flops | bytes accessed | tf_op | source)
XLA Modules:
  0.0 163.0 jit_solution(10937973517173878427)
XLA Ops:
  2.6 157.7 %embedder_window.1 = (bf16[128,3584]{1,0:T(8,128)(2,1)}, f32[32,128]{1,0:T(8,128)}) custom-call(s32[1]{0:T(128)S(6)} %copy.14.qlen_ref, s32[1]{0:T(128)S(6)} %copy.15.plen_ref, s32[1]{0:T(128)S(6)} %copy.16.pos_ref, bf16[1,64,3584]{2,1,0:T(8,128)(2,1)} %queries_ref.1, bf16[1,64,3584]{2,1,0:T(8,128)(2,1)} %passages_ref.1, f32[1,3584]{1,0:T(1,128)} %gain_hbm.1, ...), custom_call_target="tpu_custom_call" | custom-call | tf_op jit(solution)/shard_map/embedder_window/pallas_call | solution.py:518
  160.3 0.0 copy-start
  160.3 2.1 %slice_bitcast_fusion = (bf16[1,1,64,3584]{3,2,1,0:T(8,128)(2,1)}, bf16[1,1,64,3584]{3,2,1,0:T(8,128)(2,1)}) fusion(bf16[128,3584]{1,0:T(8,128)(2,1)} %get-tuple-element.5), kind=kLoop, calls=%fused_computation | loop fusion | bytes 1835008 | tf_op jit(solution)/shard_map/squeeze | solution.py:563
  162.4 0.0 copy-done
  162.4 0.6 copy.13
  (1 shorter events, 0.0 us)
Async XLA Ops:
  160.3 2.2 %copy-start = (f32[32,128]{1,0:T(8,128)S(1)}, f32[32,128]{1,0:T(8,128)}, u32[]{:S(2)}) copy-start(f32[32,128]{1,0:T(8,128)} %get-tuple-element.6) | copy-start | bytes 49156

commit v6 on v5

--- a/solution.py
+++ b/solution.py
@@ -13,10 +13,11 @@
 D, KVW, SEQ, NQ = 3584, 1024, 64, 64
 NX, NZ, NC, NY = 4, 8, 2, 4
 TEMP = 0.02
-CHUNK = 32
+CHUNK = 16
 CHUNKS = 2 * SEQ // CHUNK
 PARTS = 4
 WIDE = D // PARTS
+SLABS = NX // PARTS
 PACKS = D // 128
 FAR_X, FAR_Z = (2, 1, 3), (4, 3, 5, 2, 6, 1, 7)
 WEIGHT_ORDER = (
@@ -329,7 +330,7 @@
             stream = kept[rows, cols].astype(F32)
             square = square + jnp.sum(stream * stream, axis=-1, keepdims=True)
             gained = (stream * gain_ref[:, cols]).astype(BF)
-            v = v + jnp.dot(gained, win[n].reshape(WIDE, KVW), preferred_element_type=F32)
+            v = v + jnp.dot(gained, win[n * SLABS : (n + 1) * SLABS].reshape(WIDE, KVW), preferred_element_type=F32)
         scale = lax.rsqrt(square * (1.0 / D) + EPS)
         scales[rows, :] = jnp.broadcast_to(scale, (CHUNK, 128))
         v = v * scale
@@ -365,7 +366,7 @@
                 embed(0)
                 passage_steps[0]()
 
-            @pl.when(k == CHUNKS // 2)
+            @pl.when(k == CHUNKS * 3 // 4 - 1)
             def _():
                 passage_steps[1]()
 
@@ -446,7 +447,7 @@
             dnormed, ahead = ahead, fall(n + 1) if n + 1 < PARTS else None
             unit = kept[rows, cols].astype(F32) * scale
             both = dnormed * unit
-            gacc[:, cols] += both[0:8] + both[8:16] + both[16:24] + both[24:32]
+            gacc[:, cols] += sum(both[j : j + 8] for j in range(8, CHUNK, 8)) + both[0:8]
             res = gin[rows, cols].astype(F32) + scale * (dnormed * gain_ref[:, cols] - unit * mean)
             grad_ref[rows, cols] = res.astype(BF)
 
@@ -454,7 +455,7 @@
             def _():
                 hop(1, k, n, grad_ref, gin, seg - 1).start()
 
-        @pl.when((seg == NY - 1) & (step == 0))
+        @pl.when((seg == NY - 1) & (step == CHUNKS // 4 - 1))
         def _():
             query_steps[1]()
 

time: 163 us -> 159 us (0.975)
  Pallas kernels: 158 us -> 154 us
    pallas_call x1, Pallas kernels: 158 us -> 154 us  [local(): pl.pallas_call(kernel, out_shape=(jax.ShapeDtypeStruct((rows, D), BF), ja...]
where the time goes in v6:
time: 159 us
  Pallas kernels  154 us (97%)
  local copies, waits for them, and re-layouts  2.76 us (2%)
  between operations  2.59 us (2%)
    pallas_call x1, Pallas kernels, local(): pl.pallas_call(kernel, out_shape=(jax.ShapeDtypeStruct((rows, D), BF), ja...  154 us

profile of v6, /device:TPU:1, one launch (start us, length us, event | category | flops | bytes accessed | tf_op | source)
XLA Modules:
  0.0 158.9 jit_solution(9119088587591243014)
XLA Ops:
  2.6 153.6 %embedder_window.1 = (bf16[128,3584]{1,0:T(8,128)(2,1)}, f32[32,128]{1,0:T(8,128)}) custom-call(s32[1]{0:T(128)S(6)} %copy.14.qlen_ref, s32[1]{0:T(128)S(6)} %copy.15.plen_ref, s32[1]{0:T(128)S(6)} %copy.16.pos_ref, bf16[1,64,3584]{2,1,0:T(8,128)(2,1)} %queries_ref.1, bf16[1,64,3584]{2,1,0:T(8,128)(2,1)} %passages_ref.1, f32[1,3584]{1,0:T(1,128)} %gain_hbm.1, ...), custom_call_target="tpu_custom_call" | custom-call | tf_op jit(solution)/shard_map/embedder_window/pallas_call | solution.py:519
  156.2 0.0 copy-start
  156.2 2.1 %slice_bitcast_fusion = (bf16[1,1,64,3584]{3,2,1,0:T(8,128)(2,1)}, bf16[1,1,64,3584]{3,2,1,0:T(8,128)(2,1)}) fusion(bf16[128,3584]{1,0:T(8,128)(2,1)} %get-tuple-element.5), kind=kLoop, calls=%fused_computation | loop fusion | bytes 1835008 | tf_op jit(solution)/shard_map/squeeze | solution.py:564
  158.3 0.0 copy-done
  158.3 0.6 copy.13
  (1 shorter events, 0.0 us)
Async XLA Ops:
  156.2 2.2 %copy-start = (f32[32,128]{1,0:T(8,128)S(1)}, f32[32,128]{1,0:T(8,128)}, u32[]{:S(2)}) copy-start(f32[32,128]{1,0:T(8,128)} %get-tuple-element.6) | copy-start | bytes 49156

commit v7 on v6

--- a/solution.py
+++ b/solution.py
@@ -21,7 +21,7 @@
 PACKS = D // 128
 FAR_X, FAR_Z = (2, 1, 3), (4, 3, 5, 2, 6, 1, 7)
 WEIGHT_ORDER = (
-    2, 3, 0, 1, 2, 3, 0, 1, 2, 2, 0, 3, 2, 0, 0, 0, 2, 0, 2, 1, 0, 3, 2, 2, 0, 2, 2, 0, 0, 0, 1, 2, 2, 3, 2, 0, 1, 3,
+    2, 3, 0, 1, 0, 2, 3, 2, 0, 1, 2, 3, 0, 2, 2, 0, 1, 2, 0, 0, 0, 0, 2, 2, 2, 3, 0, 2, 2, 0, 2, 0, 1, 3, 0, 2, 1, 3,
 )
 EPS = 1e-06
 C0 = math.sqrt(2.0 / math.pi)
@@ -88,7 +88,7 @@
             rows = pl.ds(0, 48) if colour == 0 else pl.ds(48, 64)
             return win.at[xs, zs, rows, pl.ds(pl.multiple_of(pc * 512, 512), 512)]
         if tensor == W_OUT:
-            cols = pl.ds(0, 1536) if colour == 0 else pl.ds(1536, 2048)
+            cols = pl.ds(0, 1408) if colour == 0 else pl.ds(1408, 2176)
             return wout.at[xs, zs, pl.ds(pc, 1), :, cols]
         rows = pl.ds(32 * tensor, 8) if colour == 0 else pl.ds(32 * tensor + 8, 24)
         return emb.at[xs, zs, pl.ds(pc, 1), rows, :]

time: 159 us -> 156 us (0.981)
  Pallas kernels: 154 us -> 151 us
    pallas_call x1, Pallas kernels: 154 us -> 151 us  [local(): pl.pallas_call(kernel, out_shape=(jax.ShapeDtypeStruct((rows, D), BF), ja...]
where the time goes in v7:
time: 156 us
  Pallas kernels  151 us (97%)
  local copies, waits for them, and re-layouts  2.76 us (2%)
  between operations  2.59 us (2%)
    pallas_call x1, Pallas kernels, local(): pl.pallas_call(kernel, out_shape=(jax.ShapeDtypeStruct((rows, D), BF), ja...  151 us

profile of v7, /device:TPU:1, one launch (start us, length us, event | category | flops | bytes accessed | tf_op | source)
XLA Modules:
  0.0 156.3 jit_solution(14248713140984023637)
XLA Ops:
  2.6 151.0 %embedder_window.1 = (bf16[128,3584]{1,0:T(8,128)(2,1)}, f32[32,128]{1,0:T(8,128)}) custom-call(s32[1]{0:T(128)S(6)} %copy.14.qlen_ref, s32[1]{0:T(128)S(6)} %copy.15.plen_ref, s32[1]{0:T(128)S(6)} %copy.16.pos_ref, bf16[1,64,3584]{2,1,0:T(8,128)(2,1)} %queries_ref.1, bf16[1,64,3584]{2,1,0:T(8,128)(2,1)} %passages_ref.1, f32[1,3584]{1,0:T(1,128)} %gain_hbm.1, ...), custom_call_target="tpu_custom_call" | custom-call | tf_op jit(solution)/shard_map/embedder_window/pallas_call | solution.py:519
  153.6 0.0 copy-start
  153.6 2.1 %slice_bitcast_fusion = (bf16[1,1,64,3584]{3,2,1,0:T(8,128)(2,1)}, bf16[1,1,64,3584]{3,2,1,0:T(8,128)(2,1)}) fusion(bf16[128,3584]{1,0:T(8,128)(2,1)} %get-tuple-element.5), kind=kLoop, calls=%fused_computation | loop fusion | bytes 1835008 | tf_op jit(solution)/shard_map/squeeze | solution.py:564
  155.7 0.0 copy-done
  155.7 0.6 copy.13
  (1 shorter events, 0.0 us)
Async XLA Ops:
  153.6 2.2 %copy-start = (f32[32,128]{1,0:T(8,128)S(1)}, f32[32,128]{1,0:T(8,128)}, u32[]{:S(2)}) copy-start(f32[32,128]{1,0:T(8,128)} %get-tuple-element.6) | copy-start | bytes 49156

commit v8 on v7

--- a/solution.py
+++ b/solution.py
@@ -455,7 +455,7 @@
             def _():
                 hop(1, k, n, grad_ref, gin, seg - 1).start()
 
-        @pl.when((seg == NY - 1) & (step == CHUNKS // 4 - 1))
+        @pl.when((seg == NY - 1) & (step == 0))
         def _():
             query_steps[1]()
 

time: 156 us -> 155 us (level)
  Pallas kernels: 151 us -> 149 us
    pallas_call x1, Pallas kernels: 151 us -> 149 us  [local(): pl.pallas_call(kernel, out_shape=(jax.ShapeDtypeStruct((rows, D), BF), ja...]
where the time goes in v8:
time: 155 us; the launch traced here: 154 us
  Pallas kernels  149 us (96%)
  local copies, waits for them, and re-layouts  2.76 us (2%)
  between operations  2.59 us (2%)
    pallas_call x1, Pallas kernels, local(): pl.pallas_call(kernel, out_shape=(jax.ShapeDtypeStruct((rows, D), BF), ja...  149 us

profile of v8, /device:TPU:1, one launch (start us, length us, event | category | flops | bytes accessed | tf_op | source)
XLA Modules:
  0.0 154.5 jit_solution(16865974180218620901)
XLA Ops:
  2.6 149.1 %embedder_window.1 = (bf16[128,3584]{1,0:T(8,128)(2,1)}, f32[32,128]{1,0:T(8,128)}) custom-call(s32[1]{0:T(128)S(6)} %copy.14.qlen_ref, s32[1]{0:T(128)S(6)} %copy.15.plen_ref, s32[1]{0:T(128)S(6)} %copy.16.pos_ref, bf16[1,64,3584]{2,1,0:T(8,128)(2,1)} %queries_ref.1, bf16[1,64,3584]{2,1,0:T(8,128)(2,1)} %passages_ref.1, f32[1,3584]{1,0:T(1,128)} %gain_hbm.1, ...), custom_call_target="tpu_custom_call" | custom-call | tf_op jit(solution)/shard_map/embedder_window/pallas_call | solution.py:519
  151.7 0.0 copy-start
  151.7 2.1 %slice_bitcast_fusion = (bf16[1,1,64,3584]{3,2,1,0:T(8,128)(2,1)}, bf16[1,1,64,3584]{3,2,1,0:T(8,128)(2,1)}) fusion(bf16[128,3584]{1,0:T(8,128)(2,1)} %get-tuple-element.5), kind=kLoop, calls=%fused_computation | loop fusion | bytes 1835008 | tf_op jit(solution)/shard_map/squeeze | solution.py:564
  153.9 0.0 copy-done
  153.9 0.6 copy.13
  (1 shorter events, 0.0 us)
Async XLA Ops:
  151.7 2.2 %copy-start = (f32[32,128]{1,0:T(8,128)S(1)}, f32[32,128]{1,0:T(8,128)}, u32[]{:S(2)}) copy-start(f32[32,128]{1,0:T(8,128)} %get-tuple-element.6) | copy-start | bytes 49156

commit v9 on v8

--- a/solution.py
+++ b/solution.py
@@ -9,7 +9,6 @@
 
 MESH = pl.DeviceIdType.MESH
 BF, F32 = jnp.bfloat16, jnp.float32
-HI = lax.Precision.HIGHEST
 D, KVW, SEQ, NQ = 3584, 1024, 64, 64
 NX, NZ, NC, NY = 4, 8, 2, 4
 TEMP = 0.02
@@ -382,6 +381,12 @@
         for k in range(PACKS):
             embs[side, :, pl.ds(k * 128, 128)] = flat[pl.ds(32 * side + k, NQ, stride=64), :]
 
+    def product(a, b, dims):
+        a0, b0 = a.astype(BF), b.astype(BF)
+        a1, b1 = (a - a0.astype(F32)).astype(BF), (b - b0.astype(F32)).astype(BF)
+        terms = [lax.dot_general(u, v, dims, preferred_element_type=F32) for u, v in ((a0, b1), (a1, b0), (a0, b0))]
+        return terms[0] + terms[1] + terms[2]
+
     def excess(logits, onehot):
         expo = jnp.exp(logits - jnp.max(logits, axis=1, keepdims=True))
         return (expo / jnp.sum(expo, axis=1, keepdims=True) - onehot) / NQ
@@ -401,15 +406,15 @@
         passage_steps[2]()
         unpack(0)
         unit = jnp.broadcast_to(unit, (8, D))
-        logits = lax.dot_general(unit, embs[0], NT, precision=HI, preferred_element_type=F32) / TEMP
+        logits = product(unit, embs[0], NT) / TEMP
         spot = lax.broadcasted_iota(jnp.int32, (8, NQ), 1)
         dlogits = excess(logits, jnp.where(spot == pos_ref[0], 1.0, 0.0))
-        spread_back(1, jnp.dot(dlogits, embs[0], precision=HI, preferred_element_type=F32)[0:1] / TEMP)
+        spread_back(1, product(dlogits, embs[0], (((1,), (0,)), ((), ())))[0:1] / TEMP)
 
     def passages_back():
         unpack(1)
         onehot = flat[pl.ds(PACKS, NQ, stride=64), :][:, 0:NQ]
-        logits = lax.dot_general(embs[1], embs[0], NT, precision=HI, preferred_element_type=F32) / TEMP
+        logits = product(embs[1], embs[0], NT) / TEMP
         dlogits = excess(logits, onehot)
         jj = lax.broadcasted_iota(jnp.int32, (NQ, NQ), 1)
         col = jnp.sum(jnp.where(jj == me, dlogits, 0.0), axis=1, keepdims=True)

time: 155 us -> 154 us (level)
  no operation moved by 1% of the time
where the time goes in v9:
time: 154 us; the launch traced here: 153 us
  Pallas kernels  148 us (96%)
  local copies, waits for them, and re-layouts  2.76 us (2%)
  between operations  2.58 us (2%)
    pallas_call x1, Pallas kernels, local(): pl.pallas_call(kernel, out_shape=(jax.ShapeDtypeStruct((rows, D), BF), ja...  148 us

profile of v9, /device:TPU:1, one launch (start us, length us, event | category | flops | bytes accessed | tf_op | source)
XLA Modules:
  0.0 153.4 jit_solution(7684582988857187525)
XLA Ops:
  2.6 148.0 %embedder_window.1 = (bf16[128,3584]{1,0:T(8,128)(2,1)}, f32[32,128]{1,0:T(8,128)}) custom-call(s32[1]{0:T(128)S(6)} %copy.14.qlen_ref, s32[1]{0:T(128)S(6)} %copy.15.plen_ref, s32[1]{0:T(128)S(6)} %copy.16.pos_ref, bf16[1,64,3584]{2,1,0:T(8,128)(2,1)} %queries_ref.1, bf16[1,64,3584]{2,1,0:T(8,128)(2,1)} %passages_ref.1, f32[1,3584]{1,0:T(1,128)} %gain_hbm.1, ...), custom_call_target="tpu_custom_call" | custom-call | tf_op jit(solution)/shard_map/embedder_window/pallas_call | solution.py:524
  150.6 0.0 copy-start
  150.6 2.1 %slice_bitcast_fusion = (bf16[1,1,64,3584]{3,2,1,0:T(8,128)(2,1)}, bf16[1,1,64,3584]{3,2,1,0:T(8,128)(2,1)}) fusion(bf16[128,3584]{1,0:T(8,128)(2,1)} %get-tuple-element.5), kind=kLoop, calls=%fused_computation | loop fusion | bytes 1835008 | tf_op jit(solution)/shard_map/squeeze | solution.py:569
  152.8 0.0 copy-done
  152.8 0.6 copy.13
  (1 shorter events, 0.0 us)
Async XLA Ops:
  150.6 2.2 %copy-start = (f32[32,128]{1,0:T(8,128)S(1)}, f32[32,128]{1,0:T(8,128)}, u32[]{:S(2)}) copy-start(f32[32,128]{1,0:T(8,128)} %get-tuple-element.6) | copy-start | bytes 49156
